TPU v7x, 256 devices: a whole 4x4x8 slice. The times are simulated.
256 devices in a mesh: frame: 8 (over y, core), row: 4 (over z_lo), col: 8 (over z_hi, x).
Axes of the slice: x: 4, y: 4, z: 8 (z_hi: 2, z_lo: 4; z = z_hi * 4 + z_lo), core: 2. Of those that a mesh axis runs over, the one named last changes fastest.
Arguments:
- queries: bfloat16 [8, 4, 8, 384, 256], P('frame', 'row', 'col'), may hold values from -8 to 8
- key_vectors: bfloat16 [8, 4, 8, 384, 256], P('frame', 'row', 'col'), may hold values from -8 to 8
- value_vectors: bfloat16 [8, 4, 8, 384, 256], P('frame', 'row', 'col'), may hold values from -6 to 6
- forward_out: bfloat16 [8, 4, 8, 384, 256], P('frame', 'row', 'col'), may hold values from -6 to 6
- cotangent: bfloat16 [8, 4, 8, 384, 256], P('frame', 'row', 'col'), may hold values from -48 to 48
- log_norm: float32 [8, 4, 8, 2, 384], P('frame', 'row', 'col'), may hold values from 5 to 14
Outputs:
- grad_queries: bfloat16 [8, 4, 8, 384, 256], P('frame', 'row', 'col')
- grad_keys: bfloat16 [8, 4, 8, 384, 256], P('frame', 'row', 'col')
- grad_values: bfloat16 [8, 4, 8, 384, 256], P('frame', 'row', 'col')
All inputs are finite; a program needn't handle non-finite values.
Results may differ from a plain program's by a relative error of at most 0.006.
Values may be sent and summed in bfloat16 or wider, within the bound.
No kernel may reach another device: no remote copies, remote signals or barrier semaphores. Data moves between devices by JAX's collectives and lax.ppermute only.
A program may use at most 128 MiB of HBM per device.

v0:
```python
import jax
import jax.numpy as jnp
from jax import lax
from jax.sharding import PartitionSpec as P


def passed_along(x, axis, by):
    peers = lax.axis_size(axis)
    pairs = [(i, i + by) for i in range(peers) if 0 <= i + by < peers]
    return lax.ppermute(x, axis, pairs)


def with_halo(x, sides, width):
    for axis, dim in sides:
        peers, length = (lax.axis_size(axis), x.shape[dim])
        up = [(i, (i + 1) % peers) for i in range(peers - 1)]
        down = [(j, i) for i, j in up]
        last = lax.slice_in_dim(x, length - width, length, axis=dim)
        leading = lax.slice_in_dim(x, 0, width, axis=dim)
        before = lax.ppermute(last, axis, up)
        after = lax.ppermute(leading, axis, down)
        x = jnp.concatenate([before, x, after], axis=dim)
    return x


def window_valid():
    offsets = jnp.arange(3, dtype=jnp.int32) - 1
    frame_pos = lax.axis_index("frame") + offsets
    row_pos = lax.axis_index("row") + offsets
    col_pos = lax.axis_index("col") + offsets
    along_f = (frame_pos >= 0) & (frame_pos < lax.axis_size("frame"))
    along_r = (row_pos >= 0) & (row_pos < lax.axis_size("row"))
    along_c = (col_pos >= 0) & (col_pos < lax.axis_size("col"))
    return along_f[:, None, None] & along_r[None, :, None] & along_c[None, None, :]


def reduce_frame(partial_sums, dim):
    from_next = passed_along(lax.index_in_dim(partial_sums, 0, dim, keepdims=False), "frame", -1)
    from_prev = passed_along(lax.index_in_dim(partial_sums, 2, dim, keepdims=False), "frame", 1)
    return lax.index_in_dim(partial_sums, 1, dim, keepdims=False) + from_next + from_prev


def reduce_row(partial_sums, dim):
    from_next = passed_along(lax.index_in_dim(partial_sums, 0, dim, keepdims=False), "row", -1)
    from_prev = passed_along(lax.index_in_dim(partial_sums, 2, dim, keepdims=False), "row", 1)
    return lax.index_in_dim(partial_sums, 1, dim, keepdims=False) + from_next + from_prev


def reduce_col(partial_sums, dim):
    from_next = passed_along(lax.index_in_dim(partial_sums, 0, dim, keepdims=False), "col", -1)
    from_prev = passed_along(lax.index_in_dim(partial_sums, 2, dim, keepdims=False), "col", 1)
    return lax.index_in_dim(partial_sums, 1, dim, keepdims=False) + from_next + from_prev


def fold_back(partial_sums):
    partial_sums = reduce_frame(partial_sums, 0)
    partial_sums = reduce_row(partial_sums, 0)
    return reduce_col(partial_sums, 0)


def local(queries, key_vectors, value_vectors, forward_out, cotangent, log_norm):
    tile_rows = queries.shape[3]
    width = queries.shape[4]
    head_count = log_norm.shape[3]
    head_width = width // head_count
    score_scale = head_width ** (-0.5)
    valid = window_valid().reshape(9, 3)
    own_q = queries.reshape(tile_rows, head_count, head_width)
    own_do = cotangent.reshape(tile_rows, head_count, head_width)
    products = cotangent.astype(jnp.float32) * forward_out.astype(jnp.float32)
    row_delta = jnp.sum(products.reshape(tile_rows, head_count, head_width), axis=-1).T
    own_log = log_norm.reshape(head_count, tile_rows)
    out_shape = (1, 1, 1, tile_rows, width)
    joined = jnp.concatenate((key_vectors, value_vectors), axis=3)
    nearby = with_halo(joined, (("frame", 0), ("row", 1), ("col", 2)), 1)
    nearby = nearby.reshape(9, 3, 2 * tile_rows, width)

    def slab_step(grad_q, inputs):
        slab, valid_slab = inputs
        near_k = slab[:, :tile_rows].reshape(3 * tile_rows, head_count, head_width)
        near_v = slab[:, tile_rows:].reshape(3 * tile_rows, head_count, head_width)
        keep = jnp.repeat(valid_slab, tile_rows)
        scores = (
            jnp.einsum("qhd,khd->hqk", own_q, near_k, preferred_element_type=jnp.float32)
            * score_scale
        )
        probs = jnp.where(keep[None, None, :], jnp.exp(scores - own_log[:, :, None]), 0.0)
        dprobs = jnp.einsum("qhd,khd->hqk", own_do, near_v, preferred_element_type=jnp.float32)
        dscores = (probs * (dprobs - row_delta[:, :, None])).astype(jnp.bfloat16)
        grad_q = grad_q + jnp.einsum(
            "hqk,khd->qhd", dscores, near_k, preferred_element_type=jnp.float32
        )
        grad_k = jnp.einsum("hqk,qhd->khd", dscores, own_q, preferred_element_type=jnp.float32)
        grad_v = jnp.einsum(
            "hqk,qhd->khd", probs.astype(jnp.bfloat16), own_do, preferred_element_type=jnp.float32
        )
        stacked = jnp.concatenate(
            (grad_k.reshape(3, tile_rows, width), grad_v.reshape(3, tile_rows, width)), axis=1
        )
        return (grad_q, stacked)

    zeros = jnp.zeros((tile_rows, head_count, head_width), jnp.float32)
    grad_q, partial_sums = lax.scan(slab_step, zeros, (nearby, valid))
    folded = fold_back(partial_sums.reshape(3, 3, 3, 2 * tile_rows, width))
    grad_queries = grad_q.reshape(tile_rows, width) * score_scale
    grad_keys = folded[:tile_rows] * score_scale
    grad_values = folded[tile_rows:]
    return (
        grad_queries.astype(jnp.bfloat16).reshape(out_shape),
        grad_keys.astype(jnp.bfloat16).reshape(out_shape),
        grad_values.astype(jnp.bfloat16).reshape(out_shape),
    )


def solution(mesh):
    placed = (
        P("frame", "row", "col", None, None),
        P("frame", "row", "col", None, None),
        P("frame", "row", "col", None, None),
        P("frame", "row", "col", None, None),
        P("frame", "row", "col", None, None),
        P("frame", "row", "col", None, None),
    )
    return jax.shard_map(
        local,
        mesh=mesh,
        in_specs=placed,
        out_specs=(
            P("frame", "row", "col", None, None),
            P("frame", "row", "col", None, None),
            P("frame", "row", "col", None, None),
        ),
        check_vma=False,
    )
```

profile of v0, /device:TPU:168, one launch (start us, length us, event | category | flops | bytes accessed | tf_op | source)
XLA Modules:
  0.0 657.8 jit_solution(12346427803074736419)
XLA Ops:
  19.5 23.1 %collective-permute-done.3 = bf16[3,1,1,768,256]{4,3,2,1,0:T(8,128)(2,1)S(1)} collective-permute-done((bf16[3,1,1,768,256]{4,3,2,1,0:T(8,128)(2,1)S(1)}, bf16[3,1,1,768,256]{4,3,2,1,0:T(8,128)(2,1)S(1)}, u32[]{:S(2)}, u32[]{:S(2)}) %collective-permute-start.3) | collective-permute-done | bytes 1179680 | tf_op jit(solution)/shard_map/ppermute | solution.py:21
  67.5 133.1 %collective-permute-done.5 = bf16[3,3,1,768,256]{4,3,2,1,0:T(8,128)(2,1)} collective-permute-done((bf16[3,3,1,768,256]{4,3,2,1,0:T(8,128)(2,1)}, bf16[3,3,1,768,256]{4,3,2,1,0:T(8,128)(2,1)}, u32[]{:S(2)}, u32[]{:S(2)}) %collective-permute-start.5) | collective-permute-done | bytes 3538976 | tf_op jit(solution)/shard_map/ppermute | solution.py:21
  200.6 10.1 %collective-permute-done.4 = bf16[3,3,1,768,256]{4,3,2,1,0:T(8,128)(2,1)} collective-permute-done((bf16[3,3,1,768,256]{4,3,2,1,0:T(8,128)(2,1)}, bf16[3,3,1,768,256]{4,3,2,1,0:T(8,128)(2,1)}, u32[]{:S(2)}, u32[]{:S(2)}) %collective-permute-start.4) | collective-permute-done | bytes 3538976 | tf_op jit(solution)/shard_map/ppermute | solution.py:20
  210.7 8.2 %pad_maximum_fusion = bf16[3,3,3,768,256]{4,3,2,1,0:T(8,128)(2,1)} fusion(bf16[3,3,1,768,256]{4,3,2,1,0:T(8,128)(2,1)} %collective-permute-done.5, bf16[3,1,1,768,256]{4,3,2,1,0:T(8,128)(2,1)S(1)} %collective-permute-done.3, bf16[1,1,1,768,256]{4,3,2,1,0:T(8,128)(2,1)S(1)} %collective-permute-done.1, ...), kind=kLoop, calls=%fused_computation.17 | loop fusion | flops 31850496 | bytes 21233664 | tf_op jit(solution)/shard_map/concatenate | solution.py:22
  218.9 224.0 %while.13 = (s32[]{:T(128)}, f32[384,2,128]{0,2,1:T(8,128)}, f32[9,3,768,256]{3,2,1,0:T(8,128)}, bf16[9,3,768,256]{3,2,1,0:T(8,128)(2,1)}, pred[9,3]{1,0:T(8,128...) while((s32[]{:T(128)}, f32[384,2,128]{0,2,1:T(8,128)}, ...), condition=%wide.region_2.3_spmd.clone, body=%wide.region_1.2_spmd.clone.sunk | while | flops 1139441664 | bytes 44051088 | solution.py:103
  230.4 4.3 copy.42
  235.6 4.8 copy.41
  255.4 4.3 copy.42
  260.6 4.8 copy.41
  285.6 4.8 copy.41
  305.4 4.3 copy.42
  310.6 4.8 copy.41
  335.7 4.8 copy.41
  360.7 4.8 copy.41
  380.4 4.3 copy.42
  385.7 4.8 copy.41
  410.7 4.8 copy.41
  435.7 4.8 copy.41
  443.0 11.2 %fusion.17 = (f32[3,3,768,256]{3,2,1,0:T(8,128)}, f32[3,3,768,256]{3,2,1,0:T(8,128)}) fusion(f32[9,3,768,256]{3,2,1,0:T(8,128)} %get-tuple-element.52), kind=kLoop, calls=%fused_computation.46 | loop fusion | bytes 28311552 | tf_op jit(solution)/shard_map/slice | solution.py:38
  458.7 74.6 %collective-permute-done.6 = f32[3,3,768,256]{3,2,1,0:T(8,128)} collective-permute-done((f32[3,3,768,256]{3,2,1,0:T(8,128)}, f32[3,3,768,256]{3,2,1,0:T(8,128)}, u32[]{:S(2)}, u32[]{:S(2)}) %collective-permute-start.6) | collective-permute-done | bytes 7077920 | tf_op jit(solution)/shard_map/ppermute | solution.py:10
  537.1 11.3 %add_add_fusion = f32[3,3,768,256]{3,2,1,0:T(8,128)} fusion(f32[3,3,768,256]{3,2,1,0:T(8,128)} %collective-permute-done.7, f32[3,3,768,256]{3,2,1,0:T(8,128)} %collective-permute-done.6, f32[9,3,768,256]{3,2,1,0:T(8,128)} %get-tuple-element.52), kind=kLoop, calls=%fused_computation.18 | loop fusion | flops 3538944 | bytes 28311552 | tf_op jit(solution)/shard_map/add | solution.py:40
  557.2 48.2 %collective-permute-done.8 = f32[3,768,256]{2,1,0:T(8,128)S(1)} collective-permute-done((f32[3,768,256]{2,1,0:T(8,128)S(1)}, f32[3,768,256]{2,1,0:T(8,128)S(1)}, u32[]{:S(2)}, u32[]{:S(2)}) %collective-permute-start.8) | collective-permute-done | bytes 2359328 | tf_op jit(solution)/shard_map/ppermute | solution.py:10
  618.4 26.6 %collective-permute-done.10 = f32[768,256]{1,0:T(8,128)S(1)} collective-permute-done((f32[768,256]{1,0:T(8,128)}, f32[768,256]{1,0:T(8,128)S(1)}, u32[]{:S(2)}, u32[]{:S(2)}) %collective-permute-start.10) | collective-permute-done | bytes 786464 | tf_op jit(solution)/shard_map/ppermute | solution.py:10
  645.0 10.1 %collective-permute-done.11 = f32[768,256]{1,0:T(8,128)} collective-permute-done((f32[768,256]{1,0:T(8,128)}, f32[768,256]{1,0:T(8,128)}, u32[]{:S(2)}, u32[]{:S(2)}) %collective-permute-start.11) | collective-permute-done | bytes 786464 | tf_op jit(solution)/shard_map/ppermute | solution.py:10
  (199 shorter events, 239.7 us)
Async XLA Ops:
  2.5 7.2 %collective-permute-start.1 = (bf16[1,1,1,768,256]{4,3,2,1,0:T(8,128)(2,1)S(1)}, bf16[1,1,1,768,256]{4,3,2,1,0:T(8,128)(2,1)S(1)}, u32[]{:S(2)}, u32[]{:S(2)}) collective-permute-start(bf16[1,1,1,768,256]{4,3,2,1,0:T(8,128)(2,1)S(1)} %constant_dynamic-update-slice_fusion), channel_id=1, source_target_pairs={{32,0},{64,32},{96,64},{128,96},{160,128},{192,160},{224,192},{33,... | collective-permute-start | bytes 1179656 | tf_op jit(solution)/shard_map/ppermute | solution.py:21
  4.4 9.1 %collective-permute-start = (bf16[1,1,1,768,256]{4,3,2,1,0:T(8,128)(2,1)S(1)}, bf16[1,1,1,768,256]{4,3,2,1,0:T(8,128)(2,1)S(1)}, u32[]{:S(2)}, u32[]{:S(2)}) collective-permute-start(bf16[1,1,1,768,256]{4,3,2,1,0:T(8,128)(2,1)S(1)} %constant_dynamic-update-slice_fusion), channel_id=1, source_target_pairs={{0,32},{32,64},{64,96},{96,128},{128,160},{160,192},{192,224},{1,3... | collective-permute-start | bytes 1179656 | tf_op jit(solution)/shard_map/ppermute | solution.py:20
  13.7 29.0 %collective-permute-start.3 = (bf16[3,1,1,768,256]{4,3,2,1,0:T(8,128)(2,1)S(1)}, bf16[3,1,1,768,256]{4,3,2,1,0:T(8,128)(2,1)S(1)}, u32[]{:S(2)}, u32[]{:S(2)}) collective-permute-start(bf16[3,1,1,768,256]{4,3,2,1,0:T(8,128)(2,1)S(1)} %pad_maximum_fusion.2), channel_id=1, source_target_pairs={{8,0},{16,8},{24,16},{9,1},{17,9},{25,17},{10,2},{18,10},{26,18},{... | collective-permute-start | bytes 3538952 | tf_op jit(solution)/shard_map/ppermute | solution.py:21
  16.6 28.7 %collective-permute-start.2 = (bf16[3,1,1,768,256]{4,3,2,1,0:T(8,128)(2,1)S(1)}, bf16[3,1,1,768,256]{4,3,2,1,0:T(8,128)(2,1)S(1)}, u32[]{:S(2)}, u32[]{:S(2)}) collective-permute-start(bf16[3,1,1,768,256]{4,3,2,1,0:T(8,128)(2,1)S(1)} %pad_maximum_fusion.2), channel_id=1, source_target_pairs={{0,8},{8,16},{16,24},{1,9},{9,17},{17,25},{2,10},{10,18},{18,26},{... | collective-permute-start | bytes 3538952 | tf_op jit(solution)/shard_map/ppermute | solution.py:20
  47.3 153.3 %collective-permute-start.5 = (bf16[3,3,1,768,256]{4,3,2,1,0:T(8,128)(2,1)}, bf16[3,3,1,768,256]{4,3,2,1,0:T(8,128)(2,1)}, u32[]{:S(2)}, u32[]{:S(2)}) collective-permute-start(bf16[3,3,1,768,256]{4,3,2,1,0:T(8,128)(2,1)} %pad_maximum_fusion.1), channel_id=1, source_target_pairs={{1,0},{2,1},{3,2},{4,3},{5,4},{6,5},{7,6},{9,8},{10,9},{11,10},{12... | collective-permute-start | bytes 10616840 | tf_op jit(solution)/shard_map/ppermute | solution.py:21
  50.3 160.4 %collective-permute-start.4 = (bf16[3,3,1,768,256]{4,3,2,1,0:T(8,128)(2,1)}, bf16[3,3,1,768,256]{4,3,2,1,0:T(8,128)(2,1)}, u32[]{:S(2)}, u32[]{:S(2)}) collective-permute-start(bf16[3,3,1,768,256]{4,3,2,1,0:T(8,128)(2,1)} %pad_maximum_fusion.1), channel_id=1, source_target_pairs={{0,1},{1,2},{2,3},{3,4},{4,5},{5,6},{6,7},{8,9},{9,10},{10,11},{11... | collective-permute-start | bytes 10616840 | tf_op jit(solution)/shard_map/ppermute | solution.py:20
  67.5 151.4 %copy-start = (f32[1,1,1,2,384]{4,3,2,1,0:T(2,128)S(1)}, f32[1,1,1,2,384]{4,3,2,1,0:T(2,128)}, u32[]{:S(2)}) copy-start(f32[1,1,1,2,384]{4,3,2,1,0:T(2,128)} %param.13) | copy-start | bytes 9220
  454.1 79.1 %collective-permute-start.6 = (f32[3,3,768,256]{3,2,1,0:T(8,128)}, f32[3,3,768,256]{3,2,1,0:T(8,128)}, u32[]{:S(2)}, u32[]{:S(2)}) collective-permute-start(f32[3,3,768,256]{3,2,1,0:T(8,128)} %get-tuple-element.121), channel_id=1, source_target_pairs={{32,0},{64,32},{96,64},{128,96},{160,128},{192,160},{224,192},{33,... | collective-permute-start | bytes 21233672 | tf_op jit(solution)/shard_map/ppermute | solution.py:10
  456.1 81.0 %collective-permute-start.7 = (f32[3,3,768,256]{3,2,1,0:T(8,128)}, f32[3,3,768,256]{3,2,1,0:T(8,128)}, u32[]{:S(2)}, u32[]{:S(2)}) collective-permute-start(f32[3,3,768,256]{3,2,1,0:T(8,128)} %get-tuple-element.122), channel_id=1, source_target_pairs={{0,32},{32,64},{64,96},{96,128},{128,160},{160,192},{192,224},{1,3... | collective-permute-start | bytes 21233672 | tf_op jit(solution)/shard_map/ppermute | solution.py:10
  551.3 54.0 %collective-permute-start.8 = (f32[3,768,256]{2,1,0:T(8,128)S(1)}, f32[3,768,256]{2,1,0:T(8,128)S(1)}, u32[]{:S(2)}, u32[]{:S(2)}) collective-permute-start(f32[3,768,256]{2,1,0:T(8,128)S(1)} %get-tuple-element.123), channel_id=1, source_target_pairs={{8,0},{16,8},{24,16},{9,1},{17,9},{25,17},{10,2},{18,10},{26,18},{... | collective-permute-start | bytes 7077896 | tf_op jit(solution)/shard_map/ppermute | solution.py:10
  553.3 54.0 %collective-permute-start.9 = (f32[3,768,256]{2,1,0:T(8,128)S(1)}, f32[3,768,256]{2,1,0:T(8,128)S(1)}, u32[]{:S(2)}, u32[]{:S(2)}) collective-permute-start(f32[3,768,256]{2,1,0:T(8,128)S(1)} %get-tuple-element.124), channel_id=1, source_target_pairs={{0,8},{8,16},{16,24},{1,9},{9,17},{17,25},{2,10},{10,18},{18,26},{... | collective-permute-start | bytes 7077896 | tf_op jit(solution)/shard_map/ppermute | solution.py:10
  610.7 34.4 %collective-permute-start.10 = (f32[768,256]{1,0:T(8,128)}, f32[768,256]{1,0:T(8,128)S(1)}, u32[]{:S(2)}, u32[]{:S(2)}) collective-permute-start(f32[768,256]{1,0:T(8,128)} %get-tuple-element.125), channel_id=1, source_target_pairs={{1,0},{2,1},{3,2},{4,3},{5,4},{6,5},{7,6},{9,8},{10,9},{11,10},{12... | collective-permute-start | bytes 2359304 | tf_op jit(solution)/shard_map/ppermute | solution.py:10
  612.6 42.6 %collective-permute-start.11 = (f32[768,256]{1,0:T(8,128)}, f32[768,256]{1,0:T(8,128)}, u32[]{:S(2)}, u32[]{:S(2)}) collective-permute-start(f32[768,256]{1,0:T(8,128)} %get-tuple-element.126), channel_id=1, source_target_pairs={{0,1},{1,2},{2,3},{3,4},{4,5},{5,6},{6,7},{8,9},{9,10},{10,11},{11... | collective-permute-start | bytes 2359304 | tf_op jit(solution)/shard_map/ppermute | solution.py:10
where the time goes:
time: 661 us; the launch traced here: 658 us
  waiting for transfers between devices  341 us (52%)
  local copies, waits for them, and re-layouts  149 us (23%)
  matrix products  88.5 us (13%)
  other arithmetic  45.1 us (7%)
  starting transfers between devices  32.2 us (5%)
    ppermute x6, waiting for transfers between devices, passed_along(): return lax.ppermute(x, axis, pairs)  165 us
    ppermute x3, waiting for transfers between devices, with_halo(): after = lax.ppermute(leading, axis, down)  159 us
    transpose x9, local copies, waits for them, and re-layouts, slab_step(): jnp.einsum('hqk,qhd->khd', probs.astype(jnp.bfloat16), own_do, preferred_...  42.8 us
    transpose x9, local copies, waits for them, and re-layouts, slab_step(): jnp.einsum('hqk,qhd->khd', dscores, own_q, preferred_element_type=jnp.flo...  38.7 us
    dot_general x9, matrix products, slab_step(): jnp.einsum('hqk,qhd->khd', probs.astype(jnp.bfloat16), own_do, preferred_...  23.3 us
    dot_general x9, matrix products, slab_step(): jnp.einsum('hqk,khd->qhd', dscores, near_k, preferred_element_type=jnp.fl...  19.4 us
    dot_general x9, matrix products, slab_step(): jnp.einsum('qhd,khd->hqk', own_q, near_k, preferred_element_type=jnp.floa...  17.7 us
    ppermute x3, waiting for transfers between devices, with_halo(): before = lax.ppermute(last, axis, up)  16.6 us
  transfers between devices with their start and end apart: 12, of which 12 were waited for; matrix products, arithmetic and copies ran while one was open for 2% of the time, Pallas kernels for 0%

commit v1 on v0

v1 whole, which is shorter than its diff:
```python
import functools

import jax
import jax.numpy as jnp
from jax import lax
from jax.experimental import pallas as pl
from jax.experimental.pallas import tpu as pltpu
from jax.sharding import PartitionSpec as P

F32 = jnp.float32
BF16 = jnp.bfloat16
NT = (((1,), (1,)), ((), ()))
NN = (((1,), (0,)), ((), ()))
LANES = 128
VMEM_BYTES = 48 * 2**20


def dot(a, b, dims=NN):
    return lax.dot_general(a, b, dims, preferred_element_type=F32)


def shift(x, axis, by):
    peers = lax.axis_size(axis)
    pairs = [(i, i + by) for i in range(peers) if 0 <= i + by < peers]
    return lax.ppermute(x, axis, pairs)


def payload_kernel(heads, q_ref, do_ref, o_ref, log_ref, pay_ref):
    rows = q_ref.shape[0]
    blocks = rows // LANES
    for h in range(heads):
        cols = slice(h * LANES, (h + 1) * LANES)
        pay_ref[h * rows:(h + 1) * rows, :] = q_ref[:, cols]
        pay_ref[(heads + h) * rows:(heads + h + 1) * rows, :] = do_ref[:, cols]
    products = do_ref[...].astype(F32) * o_ref[...].astype(F32)
    turned = products.T
    parts = []
    for h in range(heads):
        parts += [log_ref[h:h + 1, j * LANES:(j + 1) * LANES] for j in range(blocks)]
    for h in range(heads):
        delta = jnp.sum(turned[h * LANES:(h + 1) * LANES], axis=0, keepdims=True)
        parts += [delta[:, j * LANES:(j + 1) * LANES] for j in range(blocks)]
    parts.append(jnp.zeros((16 - len(parts), LANES), F32))
    rest = jnp.concatenate(parts, axis=0)
    at = 2 * heads * rows
    for piece in range(3):
        low = rest.astype(BF16)
        pay_ref[at + 16 * piece:at + 16 * (piece + 1), :] = low
        rest = rest - low.astype(F32)


def make_payload(q, do, o, log_norm):
    rows, width = q.shape
    heads = log_norm.shape[0]
    return pl.pallas_call(
        functools.partial(payload_kernel, heads),
        out_shape=jax.ShapeDtypeStruct((2 * heads * rows + 48, LANES), BF16),
        compiler_params=pltpu.CompilerParams(vmem_limit_bytes=VMEM_BYTES),
        name="payload",
    )(q, do, o, log_norm)


def tiles_kernel(count, heads, scale, *refs):
    pays = refs[:count]
    k_ref, v_ref, dk_in, dv_in = refs[count:count + 4]
    dqs = refs[count + 4:2 * count + 4]
    dk_ref, dv_ref, kt_ref = refs[2 * count + 4:]
    rows = k_ref.shape[0]
    blocks = rows // LANES

    @pl.when(pl.program_id(0) == 0)
    def _():
        dk_ref[...] = dk_in[...]
        dv_ref[...] = dv_in[...]
        kt_ref[...] = k_ref[...].astype(F32).T.astype(BF16)

    def row_of(aux, kind):
        return jnp.concatenate([aux[kind * blocks + j:kind * blocks + j + 1] for j in range(blocks)], axis=1)

    at = 2 * heads * rows
    auxes = []
    for pay in pays:
        aux = pay[0, at:, :].astype(F32)
        auxes.append(aux[0:16] + aux[16:32] + aux[32:48])
    for h in range(heads):
        cols = slice(h * LANES, (h + 1) * LANES)
        k = k_ref[:, cols]
        v = v_ref[:, cols]
        all_p, all_ds = [], []
        for pay, aux in zip(pays, auxes):
            q = pay[0, h * rows:(h + 1) * rows, :]
            do = pay[0, (heads + h) * rows:(heads + h + 1) * rows, :]
            p = jnp.exp(dot(k, q, NT) * scale - row_of(aux, h))
            ds = p * (dot(v, do, NT) - row_of(aux, heads + h))
            all_p.append(p.astype(BF16))
            all_ds.append(ds.astype(BF16))
        p = jnp.concatenate(all_p, axis=1)
        ds = jnp.concatenate(all_ds, axis=1)
        q = jnp.concatenate([pay[0, h * rows:(h + 1) * rows, :] for pay in pays], axis=0)
        do = jnp.concatenate([pay[0, (heads + h) * rows:(heads + h + 1) * rows, :] for pay in pays], axis=0)
        dv_ref[:, cols] += dot(p, do)
        dk_ref[:, cols] += dot(ds, q)
        dq = dot(kt_ref[cols, :], ds)
        for i, dq_ref in enumerate(dqs):
            dq_ref[0, cols, :] = dq[:, i * rows:(i + 1) * rows].astype(dq_ref.dtype)


def run_tiles(pays, k, v, sums, heads, scale, kind):
    count = len(pays)
    n, pay_rows, _ = pays[0].shape
    rows, width = k.shape
    whole = pl.BlockSpec((rows, width), lambda i: (0, 0))
    pay_spec = pl.BlockSpec((1, pay_rows, LANES), lambda i: (i, 0, 0))
    dq_spec = pl.BlockSpec((1, width, rows), lambda i: (i, 0, 0))
    done = pl.pallas_call(
        functools.partial(tiles_kernel, count, heads, scale),
        grid=(n,),
        in_specs=[pay_spec] * count + [whole] * 4,
        out_specs=[dq_spec] * count + [whole] * 2,
        out_shape=[jax.ShapeDtypeStruct((n, width, rows), kind)] * count + [jax.ShapeDtypeStruct((rows, width), F32)] * 2,
        scratch_shapes=[pltpu.VMEM((width, rows), BF16)],
        input_output_aliases={count + 2: count, count + 3: count + 1},
        compiler_params=pltpu.CompilerParams(vmem_limit_bytes=VMEM_BYTES),
        cost_estimate=pl.CostEstimate(
            flops=40 * n * count * rows * rows * width // 2,
            bytes_accessed=n * count * (pay_rows * LANES * 2 + rows * width * 2),
            transcendentals=n * count * heads * rows * rows,
        ),
        name="tiles",
    )(*pays, k, v, *sums)
    return done[:count], tuple(done[count:])


def local(queries, key_vectors, value_vectors, forward_out, cotangent, log_norm):
    rows, width = queries.shape[3:]
    heads = log_norm.shape[3]
    scale = (width // heads) ** (-0.5)
    flat = (rows, width)
    k = key_vectors.reshape(flat)
    v = value_vectors.reshape(flat)
    own = make_payload(
        queries.reshape(flat), cotangent.reshape(flat), forward_out.reshape(flat), log_norm.reshape(heads, rows)
    )[None]
    sums = (jnp.zeros(flat, F32), jnp.zeros(flat, F32))
    work = functools.partial(run_tiles, k=k, v=v, heads=heads, scale=scale)

    def both(x, axis):
        return shift(x, axis, 1), shift(x, axis, -1)

    cols = both(own, "col")
    (dq_own,), sums = work([own], sums=sums, kind=F32)
    three = jnp.concatenate([own, *cols], axis=0)
    rows3 = both(three, "row")
    dq_cols, sums = work(cols, sums=sums, kind=F32)
    nine = jnp.concatenate([three, *rows3], axis=0)
    frames9 = both(nine, "frame")
    dq_rows, sums = work(rows3, sums=sums, kind=F32)
    dq_frames, sums = work(frames9, sums=sums, kind=BF16)

    from_next = shift(dq_frames[0], "frame", -1).astype(F32)
    from_prev = shift(dq_frames[1], "frame", 1).astype(F32)
    back = from_next + from_prev
    up = (dq_rows[0] + back[3:6]).astype(BF16)
    down = (dq_rows[1] + back[6:9]).astype(BF16)
    back3 = back[0:3] + shift(up, "row", -1).astype(F32) + shift(down, "row", 1).astype(F32)
    left = (dq_cols[0] + back3[1:2]).astype(BF16)
    right = (dq_cols[1] + back3[2:3]).astype(BF16)
    dq = dq_own + back3[0:1] + shift(left, "col", -1).astype(F32) + shift(right, "col", 1).astype(F32)

    dk, dv = sums
    out = queries.shape
    return (
        (dq[0].T * scale).astype(BF16).reshape(out),
        (dk * scale).astype(BF16).reshape(out),
        dv.astype(BF16).reshape(out),
    )


def solution(mesh):
    placed = P("frame", "row", "col", None, None)
    return jax.shard_map(
        local,
        mesh=mesh,
        in_specs=(placed,) * 6,
        out_specs=(placed,) * 3,
        check_vma=False,
    )
```

time: 661 us -> 197 us (0.30)
  waiting for transfers between devices: 341 us -> 132 us
  local copies, waits for them, and re-layouts: 149 us -> 4.8 us
  matrix products: 88.5 us -> 0 us
  other arithmetic: 45.1 us -> 2.03 us
  Pallas kernels: 0 us -> 24.6 us
    ppermute x12, waiting for transfers between devices: 341 us -> 132 us  [shift(): return lax.ppermute(x, axis, pairs)]
    dot_general x45 -> x0, matrix products: 88.5 us -> none  [the longest x9 23.3 us: slab_step(): jnp.einsum('hqk,qhd->khd', probs.astype(jnp.bfloat16), own_do, preferred_...]
    transpose x18 -> x0, local copies, waits for them, and re-layouts: 81.5 us -> none  [the longest x9 42.8 us: slab_step(): jnp.einsum('hqk,qhd->khd', probs.astype(jnp.bfloat16), own_do, preferred_...]
    reshape x47 -> x0, local copies, waits for them, and re-layouts: 27.9 us -> none  [the longest x9 8.5 us: slab_step(): grad_v.reshape(3, tile_rows, width)]
    pallas_call x0 -> x5, Pallas kernels: none -> 24.6 us  [the longest x4 24.4 us: run_tiles(): pl.pallas_call(functools.partial(tiles_kernel, count, heads, scale), grid...]
    squeeze x20 -> x0, local copies, waits for them, and re-layouts: 16.4 us -> none  [the longest x18 12.2 us: local(): grad_q, partial_sums = lax.scan(slab_step, zeros, (nearby, valid))]
    dynamic_update_slice x9 -> x0, other arithmetic: 14.3 us -> none  [local(): grad_q, partial_sums = lax.scan(slab_step, zeros, (nearby, valid))]
    add x3 -> x2, other arithmetic: 14.7 us -> 0.6 us  [the longest x1 0.4 us: local(): back = from_next + from_prev]
  transfers between devices with their start and end apart: 12 -> 12, of which waited for: 12 -> 12; matrix products, arithmetic and copies ran while one was open for 2% -> 1% of each run, Pallas kernels for 0% -> 4%
where the time goes in v1:
time: 197 us; the launch traced here: 196 us
  waiting for transfers between devices  132 us (67%)
  starting transfers between devices  32.1 us (16%)
  Pallas kernels  24.6 us (12%)
  local copies, waits for them, and re-layouts  4.8 us (2%)
  other arithmetic  2.03 us (1%)
    ppermute x12, waiting for transfers between devices, shift(): return lax.ppermute(x, axis, pairs)  132 us
    ppermute x12, starting transfers between devices, shift(): return lax.ppermute(x, axis, pairs)  32.1 us
    pallas_call x4, Pallas kernels, run_tiles(): pl.pallas_call(functools.partial(tiles_kernel, count, heads, scale), grid...  24.4 us
    unnamed x17, local copies, waits for them, and re-layouts  4.59 us
  transfers between devices with their start and end apart: 12, of which 12 were waited for; matrix products, arithmetic and copies ran while one was open for 1% of the time, Pallas kernels for 4%

profile of v1, /device:TPU:168, one launch (start us, length us, event | category | flops | bytes accessed | tf_op | source)
XLA Modules:
  0.0 196.3 jit_solution(12412314806359804826)
XLA Ops:
  4.3 3.7 %collective-permute-start.1 = (bf16[1,1584,128]{2,1,0:T(8,128)(2,1)S(1)}, bf16[1,1584,128]{2,1,0:T(8,128)(2,1)S(1)}, u32[]{:S(2)}, u32[]{:S(2)}) collective-permute-start(bf16[1,1584,128]{2,1,0:T(8,128)(2,1)S(1)} %bitcast.18), channel_id=1, source_target_pairs={{1,0},{2,1},{3,2},{4,3},{5,4},{6,5},{7,6},{9,8},{10,9},{11,10},{12... | collective-permute-start | bytes 1216520 | tf_op jit(solution)/shard_map/ppermute | solution.py:25
  8.0 2.1 %collective-permute-start = (bf16[1,1584,128]{2,1,0:T(8,128)(2,1)S(1)}, bf16[1,1584,128]{2,1,0:T(8,128)(2,1)S(1)}, u32[]{:S(2)}, u32[]{:S(2)}) collective-permute-start(bf16[1,1584,128]{2,1,0:T(8,128)(2,1)S(1)} %bitcast.19), channel_id=1, source_target_pairs={{0,1},{1,2},{2,3},{3,4},{4,5},{5,6},{6,7},{8,9},{9,10},{10,11},{11... | collective-permute-start | bytes 1216520 | tf_op jit(solution)/shard_map/ppermute | solution.py:25
  10.1 15.2 %collective-permute-done.1.refs_1_ = bf16[1,1584,128]{2,1,0:T(8,128)(2,1)S(1)} collective-permute-done((bf16[1,1584,128]{2,1,0:T(8,128)(2,1)S(1)}, bf16[1,1584,128]{2,1,0:T(8,128)(2,1)S(1)}, u32[]{:S(2)}, u32[]{:S(2)}) %collective-permute-start.1) | collective-permute-done | bytes 405536 | tf_op jit(solution)/shard_map/ppermute | solution.py:25
  25.3 10.3 %collective-permute-done.refs_0_ = bf16[1,1584,128]{2,1,0:T(8,128)(2,1)S(1)} collective-permute-done((bf16[1,1584,128]{2,1,0:T(8,128)(2,1)S(1)}, bf16[1,1584,128]{2,1,0:T(8,128)(2,1)S(1)}, u32[]{:S(2)}, u32[]{:S(2)}) %collective-permute-start) | collective-permute-done | bytes 405536 | tf_op jit(solution)/shard_map/ppermute | solution.py:25
  35.8 2.9 %collective-permute-start.2 = (bf16[3,1584,128]{2,1,0:T(8,128)(2,1)S(1)}, bf16[3,1584,128]{2,1,0:T(8,128)(2,1)S(1)}, u32[]{:S(2)}, u32[]{:S(2)}) collective-permute-start(bf16[3,1584,128]{2,1,0:T(8,128)(2,1)S(1)} %pad_maximum_fusion), channel_id=1, source_target_pairs={{0,8},{8,16},{16,24},{1,9},{9,17},{17,25},{2,10},{10,18},{18,26},{... | collective-permute-start | bytes 3649544 | tf_op jit(solution)/shard_map/ppermute | solution.py:25
  38.7 3.0 %collective-permute-start.3 = (bf16[3,1584,128]{2,1,0:T(8,128)(2,1)S(1)}, bf16[3,1584,128]{2,1,0:T(8,128)(2,1)S(1)}, u32[]{:S(2)}, u32[]{:S(2)}) collective-permute-start(bf16[3,1584,128]{2,1,0:T(8,128)(2,1)S(1)} %pad_maximum_fusion), channel_id=1, source_target_pairs={{8,0},{16,8},{24,16},{9,1},{17,9},{25,17},{10,2},{18,10},{26,18},{... | collective-permute-start | bytes 3649544 | tf_op jit(solution)/shard_map/ppermute | solution.py:25
  41.9 22.9 %collective-permute-done.2.refs_0_ = bf16[3,1584,128]{2,1,0:T(8,128)(2,1)S(1)} collective-permute-done((bf16[3,1584,128]{2,1,0:T(8,128)(2,1)S(1)}, bf16[3,1584,128]{2,1,0:T(8,128)(2,1)S(1)}, u32[]{:S(2)}, u32[]{:S(2)}) %collective-permute-start.2) | collective-permute-done | bytes 1216544 | tf_op jit(solution)/shard_map/ppermute | solution.py:25
  65.0 3.8 %collective-permute-done.3.refs_1_ = bf16[3,1584,128]{2,1,0:T(8,128)(2,1)S(1)} collective-permute-done((bf16[3,1584,128]{2,1,0:T(8,128)(2,1)S(1)}, bf16[3,1584,128]{2,1,0:T(8,128)(2,1)S(1)}, u32[]{:S(2)}, u32[]{:S(2)}) %collective-permute-start.3) | collective-permute-done | bytes 1216544 | tf_op jit(solution)/shard_map/ppermute | solution.py:25
  69.0 1.9 collective-permute-start.5
  70.9 2.4 %collective-permute-start.4 = (bf16[9,1584,128]{2,1,0:T(8,128)(2,1)S(1)}, bf16[9,1584,128]{2,1,0:T(8,128)(2,1)}, u32[]{:S(2)}, u32[]{:S(2)}) collective-permute-start(bf16[9,1584,128]{2,1,0:T(8,128)(2,1)S(1)} %constant_dynamic-update-slice_fusion), channel_id=1, source_target_pairs={{0,32},{32,64},{64,96},{96,128},{128,160},{160,192},{192,224},{1,3... | collective-permute-start | bytes 10948616 | tf_op jit(solution)/shard_map/ppermute | solution.py:25
  76.1 5.3 %tiles.6 = (f32[3,256,384]{2,1,0:T(8,128)S(1)}, f32[3,256,384]{2,1,0:T(8,128)S(1)}, f32[384,256]{1,0:T(8,128)S(1)}, f32[384,256]{1,0:T(8,128)S(1)}) custom-call(bf16[3,1584,128]{2,1,0:T(8,128)(2,1)S(1)} %collective-permute-done.2.refs_0_, bf16[3,1584,128]{2,1,0:T(8,128)(2,1)S(1)} %collective-permute-done.3.refs_1_, ...), custom_call_target="tpu_custom_call", output_to_operand_aliasing={{2}: (4, {}), {3}: (5, {})} | custom-call | flops 4529848320 | bytes 3612672 | tf_op jit(solution)/shard_map/tiles/pallas_call | solution.py:115
  81.4 29.7 %collective-permute-done.5.refs_1_ = bf16[9,1584,128]{2,1,0:T(8,128)(2,1)} collective-permute-done((bf16[9,1584,128]{2,1,0:T(8,128)(2,1)S(1)}, bf16[9,1584,128]{2,1,0:T(8,128)(2,1)}, u32[]{:S(2)}, u32[]{:S(2)}) %collective-permute-start.5) | collective-permute-done | bytes 3649568 | tf_op jit(solution)/shard_map/ppermute | solution.py:25
  111.1 3.9 %collective-permute-done.4.refs_0_ = bf16[9,1584,128]{2,1,0:T(8,128)(2,1)} collective-permute-done((bf16[9,1584,128]{2,1,0:T(8,128)(2,1)S(1)}, bf16[9,1584,128]{2,1,0:T(8,128)(2,1)}, u32[]{:S(2)}, u32[]{:S(2)}) %collective-permute-start.4) | collective-permute-done | bytes 3649568 | tf_op jit(solution)/shard_map/ppermute | solution.py:25
  115.0 16.4 %tiles.7 = (bf16[9,256,384]{2,1,0:T(8,128)(2,1)S(1)}, bf16[9,256,384]{2,1,0:T(8,128)(2,1)S(1)}, f32[384,256]{1,0:T(8,128)S(1)}, f32[384,256]{1,0:T(8,128)S(1)}) custom-call(bf16[9,1584,128]{2,1,0:T(8,128)(2,1)} %collective-permute-done.4.refs_0_, bf16[9,1584,128]{2,1,0:T(8,128)(2,1)} %collective-permute-done.5.refs_1_, ...), custom_call_target="tpu_custom_call", output_to_operand_aliasing={{2}: (4, {}), {3}: (5, {})} | custom-call | flops 13589544960 | bytes 10838016 | tf_op jit(solution)/shard_map/tiles/pallas_call | solution.py:115
  133.4 2.4 %collective-permute-start.7 = (bf16[9,256,384]{2,1,0:T(8,128)(2,1)S(1)}, bf16[9,256,384]{2,1,0:T(8,128)(2,1)S(1)}, u32[]{:S(2)}, u32[]{:S(2)}) collective-permute-start(bf16[9,256,384]{2,1,0:T(8,128)(2,1)S(1)} %get-tuple-element.26), channel_id=1, source_target_pairs={{0,32},{32,64},{64,96},{96,128},{128,160},{160,192},{192,224},{1,3... | collective-permute-start | bytes 5308424 | tf_op jit(solution)/shard_map/ppermute | solution.py:25
  135.8 17.6 %collective-permute-done.6 = bf16[9,256,384]{2,1,0:T(8,128)(2,1)S(1)} collective-permute-done((bf16[9,256,384]{2,1,0:T(8,128)(2,1)S(1)}, bf16[9,256,384]{2,1,0:T(8,128)(2,1)S(1)}, u32[]{:S(2)}, u32[]{:S(2)}) %collective-permute-start.6) | collective-permute-done | bytes 1769504 | tf_op jit(solution)/shard_map/ppermute | solution.py:25
  153.4 3.8 %collective-permute-done.7 = bf16[9,256,384]{2,1,0:T(8,128)(2,1)S(1)} collective-permute-done((bf16[9,256,384]{2,1,0:T(8,128)(2,1)S(1)}, bf16[9,256,384]{2,1,0:T(8,128)(2,1)S(1)}, u32[]{:S(2)}, u32[]{:S(2)}) %collective-permute-start.7) | collective-permute-done | bytes 1769504 | tf_op jit(solution)/shard_map/ppermute | solution.py:25
  157.9 2.2 %collective-permute-start.8 = (bf16[3,256,384]{2,1,0:T(8,128)(2,1)S(1)}, bf16[3,256,384]{2,1,0:T(8,128)(2,1)S(1)}, u32[]{:S(2)}, u32[]{:S(2)}) collective-permute-start(bf16[3,256,384]{2,1,0:T(8,128)(2,1)S(1)} %get-tuple-element.36), channel_id=1, source_target_pairs={{8,0},{16,8},{24,16},{9,1},{17,9},{25,17},{10,2},{18,10},{26,18},{... | collective-permute-start | bytes 1769480 | tf_op jit(solution)/shard_map/ppermute | solution.py:25
  160.2 3.6 %collective-permute-start.9 = (bf16[3,256,384]{2,1,0:T(8,128)(2,1)S(1)}, bf16[3,256,384]{2,1,0:T(8,128)(2,1)S(1)}, u32[]{:S(2)}, u32[]{:S(2)}) collective-permute-start(bf16[3,256,384]{2,1,0:T(8,128)(2,1)S(1)} %get-tuple-element.37), channel_id=1, source_target_pairs={{0,8},{8,16},{16,24},{1,9},{9,17},{17,25},{2,10},{10,18},{18,26},{... | collective-permute-start | bytes 1769480 | tf_op jit(solution)/shard_map/ppermute | solution.py:25
  163.8 10.5 %collective-permute-done.8 = bf16[3,256,384]{2,1,0:T(8,128)(2,1)S(1)} collective-permute-done((bf16[3,256,384]{2,1,0:T(8,128)(2,1)S(1)}, bf16[3,256,384]{2,1,0:T(8,128)(2,1)S(1)}, u32[]{:S(2)}, u32[]{:S(2)}) %collective-permute-start.8) | collective-permute-done | bytes 589856 | tf_op jit(solution)/shard_map/ppermute | solution.py:25
  174.3 1.9 collective-permute-done.9
  178.4 3.9 %collective-permute-start.11 = (bf16[1,256,384]{2,1,0:T(8,128)(2,1)S(1)}, bf16[1,256,384]{2,1,0:T(8,128)(2,1)S(1)}, u32[]{:S(2)}, u32[]{:S(2)}) collective-permute-start(bf16[1,256,384]{2,1,0:T(8,128)(2,1)S(1)} %get-tuple-element.39), channel_id=1, source_target_pairs={{0,1},{1,2},{2,3},{3,4},{4,5},{5,6},{6,7},{8,9},{9,10},{10,11},{11... | collective-permute-start | bytes 589832 | tf_op jit(solution)/shard_map/ppermute | solution.py:25
  183.2 2.1 %collective-permute-done.10 = bf16[1,256,384]{2,1,0:T(8,128)(2,1)S(1)} collective-permute-done((bf16[1,256,384]{2,1,0:T(8,128)(2,1)S(1)}, bf16[1,256,384]{2,1,0:T(8,128)(2,1)S(1)}, u32[]{:S(2)}, u32[]{:S(2)}) %collective-permute-start.10) | collective-permute-done | bytes 196640 | tf_op jit(solution)/shard_map/ppermute | solution.py:25
  185.2 10.1 %collective-permute-done.11 = bf16[1,256,384]{2,1,0:T(8,128)(2,1)S(1)} collective-permute-done((bf16[1,256,384]{2,1,0:T(8,128)(2,1)S(1)}, bf16[1,256,384]{2,1,0:T(8,128)(2,1)S(1)}, u32[]{:S(2)}, u32[]{:S(2)}) %collective-permute-start.11) | collective-permute-done | bytes 196640 | tf_op jit(solution)/shard_map/ppermute | solution.py:25
  (32 shorter events, 13.5 us)
Async XLA Ops:
  0.6 0.9 copy-start
  1.6 0.9 copy-start.1
  2.5 0.9 copy-start.2
  3.4 0.7 copy-start.3
  4.3 21.1 %collective-permute-start.1 = (bf16[1,1584,128]{2,1,0:T(8,128)(2,1)S(1)}, bf16[1,1584,128]{2,1,0:T(8,128)(2,1)S(1)}, u32[]{:S(2)}, u32[]{:S(2)}) collective-permute-start(bf16[1,1584,128]{2,1,0:T(8,128)(2,1)S(1)} %bitcast.18), channel_id=1, source_target_pairs={{1,0},{2,1},{3,2},{4,3},{5,4},{6,5},{7,6},{9,8},{10,9},{11,10},{12... | collective-permute-start | bytes 1216520 | tf_op jit(solution)/shard_map/ppermute | solution.py:25
  8.0 27.6 %collective-permute-start = (bf16[1,1584,128]{2,1,0:T(8,128)(2,1)S(1)}, bf16[1,1584,128]{2,1,0:T(8,128)(2,1)S(1)}, u32[]{:S(2)}, u32[]{:S(2)}) collective-permute-start(bf16[1,1584,128]{2,1,0:T(8,128)(2,1)S(1)} %bitcast.19), channel_id=1, source_target_pairs={{0,1},{1,2},{2,3},{3,4},{4,5},{5,6},{6,7},{8,9},{9,10},{10,11},{11... | collective-permute-start | bytes 1216520 | tf_op jit(solution)/shard_map/ppermute | solution.py:25
  35.8 29.0 %collective-permute-start.2 = (bf16[3,1584,128]{2,1,0:T(8,128)(2,1)S(1)}, bf16[3,1584,128]{2,1,0:T(8,128)(2,1)S(1)}, u32[]{:S(2)}, u32[]{:S(2)}) collective-permute-start(bf16[3,1584,128]{2,1,0:T(8,128)(2,1)S(1)} %pad_maximum_fusion), channel_id=1, source_target_pairs={{0,8},{8,16},{16,24},{1,9},{9,17},{17,25},{2,10},{10,18},{18,26},{... | collective-permute-start | bytes 3649544 | tf_op jit(solution)/shard_map/ppermute | solution.py:25
  38.7 30.1 %collective-permute-start.3 = (bf16[3,1584,128]{2,1,0:T(8,128)(2,1)S(1)}, bf16[3,1584,128]{2,1,0:T(8,128)(2,1)S(1)}, u32[]{:S(2)}, u32[]{:S(2)}) collective-permute-start(bf16[3,1584,128]{2,1,0:T(8,128)(2,1)S(1)} %pad_maximum_fusion), channel_id=1, source_target_pairs={{8,0},{16,8},{24,16},{9,1},{17,9},{25,17},{10,2},{18,10},{26,18},{... | collective-permute-start | bytes 3649544 | tf_op jit(solution)/shard_map/ppermute | solution.py:25
  65.0 8.4 %copy-start.4 = (bf16[1,1,1,384,256]{4,3,2,1,0:T(8,128)(2,1)S(1)}, bf16[1,1,1,384,256]{4,3,2,1,0:T(8,128)(2,1)}, u32[]{:S(2)}) copy-start(bf16[1,1,1,384,256]{4,3,2,1,0:T(8,128)(2,1)} %param.7) | copy-start | bytes 589828
  65.0 8.4 %copy-start.5 = (bf16[1,1,1,384,256]{4,3,2,1,0:T(8,128)(2,1)S(1)}, bf16[1,1,1,384,256]{4,3,2,1,0:T(8,128)(2,1)}, u32[]{:S(2)}) copy-start(bf16[1,1,1,384,256]{4,3,2,1,0:T(8,128)(2,1)} %param.8) | copy-start | bytes 589828
  69.0 42.1 %collective-permute-start.5 = (bf16[9,1584,128]{2,1,0:T(8,128)(2,1)S(1)}, bf16[9,1584,128]{2,1,0:T(8,128)(2,1)}, u32[]{:S(2)}, u32[]{:S(2)}) collective-permute-start(bf16[9,1584,128]{2,1,0:T(8,128)(2,1)S(1)} %constant_dynamic-update-slice_fusion), channel_id=1, source_target_pairs={{32,0},{64,32},{96,64},{128,96},{160,128},{192,160},{224,192},{33,... | collective-permute-start | bytes 10948616 | tf_op jit(solution)/shard_map/ppermute | solution.py:25
  70.9 44.1 %collective-permute-start.4 = (bf16[9,1584,128]{2,1,0:T(8,128)(2,1)S(1)}, bf16[9,1584,128]{2,1,0:T(8,128)(2,1)}, u32[]{:S(2)}, u32[]{:S(2)}) collective-permute-start(bf16[9,1584,128]{2,1,0:T(8,128)(2,1)S(1)} %constant_dynamic-update-slice_fusion), channel_id=1, source_target_pairs={{0,32},{32,64},{64,96},{96,128},{128,160},{160,192},{192,224},{1,3... | collective-permute-start | bytes 10948616 | tf_op jit(solution)/shard_map/ppermute | solution.py:25
  131.4 21.9 %collective-permute-start.6 = (bf16[9,256,384]{2,1,0:T(8,128)(2,1)S(1)}, bf16[9,256,384]{2,1,0:T(8,128)(2,1)S(1)}, u32[]{:S(2)}, u32[]{:S(2)}) collective-permute-start(bf16[9,256,384]{2,1,0:T(8,128)(2,1)S(1)} %get-tuple-element.25), channel_id=1, source_target_pairs={{32,0},{64,32},{96,64},{128,96},{160,128},{192,160},{224,192},{33,... | collective-permute-start | bytes 5308424 | tf_op jit(solution)/shard_map/ppermute | solution.py:25
  133.4 23.8 %collective-permute-start.7 = (bf16[9,256,384]{2,1,0:T(8,128)(2,1)S(1)}, bf16[9,256,384]{2,1,0:T(8,128)(2,1)S(1)}, u32[]{:S(2)}, u32[]{:S(2)}) collective-permute-start(bf16[9,256,384]{2,1,0:T(8,128)(2,1)S(1)} %get-tuple-element.26), channel_id=1, source_target_pairs={{0,32},{32,64},{64,96},{96,128},{128,160},{160,192},{192,224},{1,3... | collective-permute-start | bytes 5308424 | tf_op jit(solution)/shard_map/ppermute | solution.py:25
  157.9 16.3 %collective-permute-start.8 = (bf16[3,256,384]{2,1,0:T(8,128)(2,1)S(1)}, bf16[3,256,384]{2,1,0:T(8,128)(2,1)S(1)}, u32[]{:S(2)}, u32[]{:S(2)}) collective-permute-start(bf16[3,256,384]{2,1,0:T(8,128)(2,1)S(1)} %get-tuple-element.36), channel_id=1, source_target_pairs={{8,0},{16,8},{24,16},{9,1},{17,9},{25,17},{10,2},{18,10},{26,18},{... | collective-permute-start | bytes 1769480 | tf_op jit(solution)/shard_map/ppermute | solution.py:25
  160.2 16.1 %collective-permute-start.9 = (bf16[3,256,384]{2,1,0:T(8,128)(2,1)S(1)}, bf16[3,256,384]{2,1,0:T(8,128)(2,1)S(1)}, u32[]{:S(2)}, u32[]{:S(2)}) collective-permute-start(bf16[3,256,384]{2,1,0:T(8,128)(2,1)S(1)} %get-tuple-element.37), channel_id=1, source_target_pairs={{0,8},{8,16},{16,24},{1,9},{9,17},{17,25},{2,10},{10,18},{18,26},{... | collective-permute-start | bytes 1769480 | tf_op jit(solution)/shard_map/ppermute | solution.py:25
  176.5 8.7 %collective-permute-start.10 = (bf16[1,256,384]{2,1,0:T(8,128)(2,1)S(1)}, bf16[1,256,384]{2,1,0:T(8,128)(2,1)S(1)}, u32[]{:S(2)}, u32[]{:S(2)}) collective-permute-start(bf16[1,256,384]{2,1,0:T(8,128)(2,1)S(1)} %get-tuple-element.38), channel_id=1, source_target_pairs={{1,0},{2,1},{3,2},{4,3},{5,4},{6,5},{7,6},{9,8},{10,9},{11,10},{12... | collective-permute-start | bytes 589832 | tf_op jit(solution)/shard_map/ppermute | solution.py:25
  178.4 16.9 %collective-permute-start.11 = (bf16[1,256,384]{2,1,0:T(8,128)(2,1)S(1)}, bf16[1,256,384]{2,1,0:T(8,128)(2,1)S(1)}, u32[]{:S(2)}, u32[]{:S(2)}) collective-permute-start(bf16[1,256,384]{2,1,0:T(8,128)(2,1)S(1)} %get-tuple-element.39), channel_id=1, source_target_pairs={{0,1},{1,2},{2,3},{3,4},{4,5},{5,6},{6,7},{8,9},{9,10},{10,11},{11... | collective-permute-start | bytes 589832 | tf_op jit(solution)/shard_map/ppermute | solution.py:25

commit v2 on v1

v2 whole, which is shorter than its diff:
```python
import functools

import jax
import jax.numpy as jnp
from jax import lax
from jax.experimental import pallas as pl
from jax.experimental.pallas import tpu as pltpu
from jax.sharding import PartitionSpec as P

F32 = jnp.float32
BF16 = jnp.bfloat16
NT = (((1,), (1,)), ((), ()))
NN = (((1,), (0,)), ((), ()))
LANES = 128
VMEM_BYTES = 36 * 2**20


def dot(a, b, dims=NN):
    return lax.dot_general(a, b, dims, preferred_element_type=F32)


def meet(x, axis, second):
    pairs = []
    for i in range(second, lax.axis_size(axis) - 1, 2):
        pairs += [(i, i + 1), (i + 1, i)]
    return lax.ppermute(x, axis, pairs)


def payload_kernel(heads, q_ref, do_ref, o_ref, log_ref, k_ref, v_ref, pay_ref, kv_ref):
    rows = q_ref.shape[0]
    blocks = rows // LANES
    kv_ref[0] = k_ref[...]
    kv_ref[1] = v_ref[...]
    for h in range(heads):
        cols = slice(h * LANES, (h + 1) * LANES)
        pay_ref[0, h * rows:(h + 1) * rows, :] = q_ref[:, cols]
        pay_ref[0, (heads + h) * rows:(heads + h + 1) * rows, :] = do_ref[:, cols]
    products = do_ref[...].astype(F32) * o_ref[...].astype(F32)
    turned = products.T
    parts = []
    for h in range(heads):
        parts += [log_ref[h:h + 1, j * LANES:(j + 1) * LANES] for j in range(blocks)]
    for h in range(heads):
        delta = jnp.sum(turned[h * LANES:(h + 1) * LANES], axis=0, keepdims=True)
        parts += [delta[:, j * LANES:(j + 1) * LANES] for j in range(blocks)]
    parts.append(jnp.zeros((16 - len(parts), LANES), F32))
    rest = jnp.concatenate(parts, axis=0)
    at = 2 * heads * rows
    for piece in range(3):
        low = rest.astype(BF16)
        pay_ref[0, at + 16 * piece:at + 16 * (piece + 1), :] = low
        rest = rest - low.astype(F32)


def make_payloads(q, do, o, log_norm, k, v):
    rows, width = q.shape
    heads = log_norm.shape[0]
    return pl.pallas_call(
        functools.partial(payload_kernel, heads),
        out_shape=[
            jax.ShapeDtypeStruct((1, 2 * heads * rows + 48, LANES), BF16),
            jax.ShapeDtypeStruct((2, rows, width), BF16),
        ],
        compiler_params=pltpu.CompilerParams(vmem_limit_bytes=60 * 2**20),
        name="payloads",
    )(q, do, o, log_norm, k, v)


def tiles_kernel(count, sides, heads, scale, more_dq, more_acc, *refs):
    pays, refs = refs[:count], refs[count:]
    kvs, refs = refs[:sides], refs[sides:]
    dq_ins, refs = (refs[:count], refs[count:]) if more_dq else (None, refs)
    acc_ins, refs = (refs[:sides], refs[sides:]) if more_acc else (None, refs)
    dqs, refs = refs[:count], refs[count:]
    accs, kt_ref = refs[:sides], refs[sides]
    rows = kvs[0].shape[1]
    blocks = rows // LANES

    @pl.when(pl.program_id(0) == 0)
    def _():
        for s in range(sides):
            accs[s][...] = acc_ins[s][...] if more_acc else jnp.zeros_like(accs[s])
            kt_ref[:, s * rows:(s + 1) * rows] = kvs[s][0].astype(F32).T.astype(BF16)

    def row_of(aux, kind):
        return jnp.concatenate([aux[kind * blocks + j:kind * blocks + j + 1] for j in range(blocks)], axis=1)

    at = 2 * heads * rows
    auxes = []
    for pay in pays:
        aux = pay[0, at:, :].astype(F32)
        auxes.append(aux[0:16] + aux[16:32] + aux[32:48])
    for h in range(heads):
        cols = slice(h * LANES, (h + 1) * LANES)
        q = jnp.concatenate([pay[0, h * rows:(h + 1) * rows, :] for pay in pays], axis=0)
        do = jnp.concatenate([pay[0, (heads + h) * rows:(heads + h + 1) * rows, :] for pay in pays], axis=0)
        log = jnp.concatenate([row_of(aux, h) for aux in auxes], axis=1)
        delta = jnp.concatenate([row_of(aux, heads + h) for aux in auxes], axis=1)
        dq = None
        for s in range(sides):
            k = kvs[s][0, :, cols]
            v = kvs[s][1, :, cols]
            p = jnp.exp(dot(k, q, NT) * scale - log)
            ds = (p * (dot(v, do, NT) - delta)).astype(BF16)
            accs[s][1, :, cols] += dot(p.astype(BF16), do)
            accs[s][0, :, cols] += dot(ds, q)
            part = dot(kt_ref[cols, s * rows:(s + 1) * rows], ds)
            dq = part if dq is None else dq + part
        for i in range(count):
            mine = dq[:, i * rows:(i + 1) * rows]
            if more_dq:
                mine = mine + dq_ins[i][0, cols, :]
            dqs[i][0, cols, :] = mine.astype(dqs[i].dtype)


def run_tiles(pays, kvs, heads, scale, kinds, acc_kind=F32, dq_in=(), acc_in=()):
    count, sides = len(pays), len(kvs)
    n, pay_rows, _ = pays[0].shape
    _, rows, width = kvs[0].shape
    whole = pl.BlockSpec((2, rows, width), lambda i: (0, 0, 0))
    pay_spec = pl.BlockSpec((1, pay_rows, LANES), lambda i: (i, 0, 0))
    dq_spec = pl.BlockSpec((1, width, rows), lambda i: (i, 0, 0))
    done = pl.pallas_call(
        functools.partial(tiles_kernel, count, sides, heads, scale, bool(dq_in), bool(acc_in)),
        grid=(n,),
        in_specs=[pay_spec] * count + [whole] * sides + [dq_spec] * len(dq_in) + [whole] * len(acc_in),
        out_specs=[dq_spec] * count + [whole] * sides,
        out_shape=[jax.ShapeDtypeStruct((n, width, rows), kind) for kind in kinds]
        + [jax.ShapeDtypeStruct((2, rows, width), F32)] * sides,
        scratch_shapes=[pltpu.VMEM((width, sides * rows), BF16)],
        compiler_params=pltpu.CompilerParams(vmem_limit_bytes=VMEM_BYTES),
        cost_estimate=pl.CostEstimate(
            flops=20 * n * count * sides * rows * rows * width,
            bytes_accessed=n * count * (pay_rows * LANES * 2 + rows * width * 2),
            transcendentals=n * count * sides * heads * rows * rows,
        ),
        name="tiles",
    )(*pays, *kvs, *dq_in, *acc_in)
    return done[:count], done[count:]


def local(queries, key_vectors, value_vectors, forward_out, cotangent, log_norm):
    rows, width = queries.shape[3:]
    heads = log_norm.shape[3]
    scale = (width // heads) ** (-0.5)
    flat = (rows, width)
    own, own_kv = make_payloads(
        queries.reshape(flat),
        cotangent.reshape(flat),
        forward_out.reshape(flat),
        log_norm.reshape(heads, rows),
        key_vectors.reshape(flat),
        value_vectors.reshape(flat),
    )

    kv_b = meet(own_kv, "col", 1)
    kv_a = meet(own_kv, "col", 0)
    row_b = meet(own, "row", 1)
    row_a = meet(own, "row", 0)
    frame_b = meet(own, "frame", 1)
    frame_a = meet(own, "frame", 0)
    pair = jnp.concatenate([row_a, row_b], axis=0)
    pair_b = meet(pair, "frame", 1)
    pair_a = meet(pair, "frame", 0)

    work = functools.partial(run_tiles, heads=heads, scale=scale)
    near = [own, row_a, row_b, frame_a, frame_b]
    dqs, (acc_own,) = work(near, [own_kv], kinds=[F32] * 5)
    dqs, acc_ab = work(near, [kv_a, kv_b], dq_in=dqs, kinds=[F32] * 3 + [BF16] * 2)
    dq_own, dq_row_a, dq_row_b, dq_frame_a, dq_frame_b = dqs
    far_dqs, accs = work(
        [pair_a, pair_b], [own_kv, kv_a, kv_b], acc_in=(acc_own, *acc_ab), kinds=[BF16] * 2
    )

    own_back_b = meet(dq_frame_b, "frame", 1).astype(F32)
    own_back_a = meet(dq_frame_a, "frame", 0).astype(F32)
    pair_back = meet(far_dqs[1], "frame", 1).astype(F32) + meet(far_dqs[0], "frame", 0).astype(F32)
    dkv_b = meet(accs[2].astype(BF16), "col", 1).astype(F32)
    dkv_a = meet(accs[1].astype(BF16), "col", 0).astype(F32)
    row_back_b = meet((dq_row_b + pair_back[1:2]).astype(BF16), "row", 1).astype(F32)
    row_back_a = meet((dq_row_a + pair_back[0:1]).astype(BF16), "row", 0).astype(F32)
    dq = dq_own + own_back_a + own_back_b + row_back_a + row_back_b
    dkv = accs[0] + dkv_a + dkv_b

    out = queries.shape
    return (
        (dq[0].T * scale).astype(BF16).reshape(out),
        (dkv[0] * scale).astype(BF16).reshape(out),
        dkv[1].astype(BF16).reshape(out),
    )


def solution(mesh):
    placed = P("frame", "row", "col", None, None)
    return jax.shard_map(
        local,
        mesh=mesh,
        in_specs=(placed,) * 6,
        out_specs=(placed,) * 3,
        check_vma=False,
    )
```

time: 197 us -> 90.2 us (0.46)
  the two profiles are of different devices: /device:TPU:168 before, /device:TPU:46 now
where the time goes in v2:
time: 90.2 us; the launch traced here: 89.9 us
  starting transfers between devices  37.2 us (41%)
  waiting for transfers between devices  24.7 us (27%)
  Pallas kernels  24.3 us (27%)
  local copies, waits for them, and re-layouts  1.61 us (2%)
  other arithmetic  1.21 us (1%)
    ppermute x16, starting transfers between devices, meet(): return lax.ppermute(x, axis, pairs)  37.2 us
    ppermute x16, waiting for transfers between devices, meet(): return lax.ppermute(x, axis, pairs)  24.7 us
    pallas_call x3, Pallas kernels, run_tiles(): pl.pallas_call(functools.partial(tiles_kernel, count, sides, heads, scale...  21.9 us
    pallas_call x1, Pallas kernels, make_payloads(): pl.pallas_call(functools.partial(payload_kernel, heads), out_shape=[jax.S...  2.38 us
  transfers between devices with their start and end apart: 16, of which 5 were waited for; matrix products, arithmetic and copies ran while one was open for 2% of the time, Pallas kernels for 13%

profile of v2, /device:TPU:46, one launch (start us, length us, event | category | flops | bytes accessed | tf_op | source)
XLA Modules:
  0.0 89.9 jit_solution(12362721508999106898)
XLA Ops:
  0.6 2.4 %payloads.1 = (bf16[1,1584,128]{2,1,0:T(8,128)(2,1)}, bf16[2,384,256]{2,1,0:T(8,128)(2,1)}) custom-call(bf16[384,256]{1,0:T(8,128)(2,1)} %bitcast.16, bf16[384,256]{1,0:T(8,128)(2,1)} %bitcast.17, bf16[384,256]{1,0:T(8,128)(2,1)} %bitcast.18, f32[2,384]{1,0:T(2,128)} %bitcast.21, bf16[384,256]{1,0:T(8,128)(2,1)} %bitcast.19, bf16[384,256]{1,0:T(8,128)(2,1)} %bitcast.20), custom_call_target="tpu_custom_call" | custom-call | tf_op jit(solution)/shard_map/payloads/pallas_call | solution.py:58
  3.0 0.1 collective-permute-start
  3.1 5.6 %collective-permute-start.1 = (bf16[1,1584,128]{2,1,0:T(8,128)(2,1)}, bf16[1,1584,128]{2,1,0:T(8,128)(2,1)S(1)}, u32[]{:S(2)}, u32[]{:S(2)}) collective-permute-start(bf16[1,1584,128]{2,1,0:T(8,128)(2,1)} %get-tuple-element.23.refs_0_), channel_id=1, source_target_pairs={{8,16},{16,8},{9,17},{17,9},{10,18},{18,10},{11,19},{19,11},{12,20... | collective-permute-start | bytes 1216520 | tf_op jit(solution)/shard_map/ppermute | solution.py:26
  8.9 2.4 %collective-permute-start.3 = (bf16[1,1584,128]{2,1,0:T(8,128)(2,1)}, bf16[1,1584,128]{2,1,0:T(8,128)(2,1)S(1)}, u32[]{:S(2)}, u32[]{:S(2)}) collective-permute-start(bf16[1,1584,128]{2,1,0:T(8,128)(2,1)} %get-tuple-element.23.refs_0_), channel_id=1, source_target_pairs={{32,64},{64,32},{96,128},{128,96},{160,192},{192,160},{33,65},{65,... | collective-permute-start | bytes 1216520 | tf_op jit(solution)/shard_map/ppermute | solution.py:26
  11.3 0.9 %collective-permute-start.4 = (bf16[2,384,256]{2,1,0:T(8,128)(2,1)}, bf16[2,384,256]{2,1,0:T(8,128)(2,1)S(1)}, u32[]{:S(2)}, u32[]{:S(2)}) collective-permute-start(bf16[2,384,256]{2,1,0:T(8,128)(2,1)} %get-tuple-element.24.refs_5_.refs_2_), channel_id=1, source_target_pairs={{0,1},{1,0},{2,3},{3,2},{4,5},{5,4},{6,7},{7,6},{8,9},{9,8},{10,11... | collective-permute-start | bytes 1179656 | tf_op jit(solution)/shard_map/ppermute | solution.py:26
  12.2 2.1 %collective-permute-done.refs_1_ = bf16[1,1584,128]{2,1,0:T(8,128)(2,1)S(1)} collective-permute-done((bf16[1,1584,128]{2,1,0:T(8,128)(2,1)}, bf16[1,1584,128]{2,1,0:T(8,128)(2,1)S(1)}, u32[]{:S(2)}, u32[]{:S(2)}) %collective-permute-start) | collective-permute-done | bytes 405536 | tf_op jit(solution)/shard_map/ppermute | solution.py:26
  14.3 8.1 %collective-permute-start.5 = (bf16[2,384,256]{2,1,0:T(8,128)(2,1)}, bf16[2,384,256]{2,1,0:T(8,128)(2,1)S(1)}, u32[]{:S(2)}, u32[]{:S(2)}) collective-permute-start(bf16[2,384,256]{2,1,0:T(8,128)(2,1)} %get-tuple-element.24.refs_5_.refs_2_), channel_id=1, source_target_pairs={{1,2},{2,1},{3,4},{4,3},{5,6},{6,5},{9,10},{10,9},{11,12},{12,11},... | collective-permute-start | bytes 1179656 | tf_op jit(solution)/shard_map/ppermute | solution.py:26
  22.7 2.6 %collective-permute-start.9 = (bf16[2,1584,128]{2,1,0:T(8,128)(2,1)S(1)}, bf16[2,1584,128]{2,1,0:T(8,128)(2,1)S(1)}, u32[]{:S(2)}, u32[]{:S(2)}) collective-permute-start(bf16[2,1584,128]{2,1,0:T(8,128)(2,1)S(1)} %constant_dynamic-update-slice_fusion), channel_id=1, source_target_pairs={{32,64},{64,32},{96,128},{128,96},{160,192},{192,160},{33,65},{65,... | collective-permute-start | bytes 2433032 | tf_op jit(solution)/shard_map/ppermute | solution.py:26
  25.4 4.0 %tiles.3 = (f32[1,256,384]{2,1,0:T(8,128)S(1)}, f32[1,256,384]{2,1,0:T(8,128)S(1)}, f32[1,256,384]{2,1,0:T(8,128)S(1)}, f32[1,256,384]{2,1,0:T(8,128)S(1)}, f32[...) custom-call(bf16[1,1584,128]{2,1,0:T(8,128)(2,1)S(1)} %copy-done, ...), custom_call_target="tpu_custom_call" | custom-call | flops 3774873600 | bytes 3010560 | tf_op jit(solution)/shard_map/tiles/pallas_call | solution.py:123
  29.3 11.5 %collective-permute-done.5.refs_6_.refs_4_ = bf16[2,384,256]{2,1,0:T(8,128)(2,1)S(1)} collective-permute-done((bf16[2,384,256]{2,1,0:T(8,128)(2,1)}, bf16[2,384,256]{2,1,0:T(8,128)(2,1)S(1)}, u32[]{:S(2)}, u32[]{:S(2)}) %collective-permute-start.5) | collective-permute-done | bytes 393248 | tf_op jit(solution)/shard_map/ppermute | solution.py:26
  40.9 7.9 %tiles.4 = (f32[1,256,384]{2,1,0:T(8,128)S(1)}, f32[1,256,384]{2,1,0:T(8,128)S(1)}, f32[1,256,384]{2,1,0:T(8,128)S(1)}, bf16[1,256,384]{2,1,0:T(8,128)(2,1)S(1)}...) custom-call(bf16[1,1584,128]{2,1,0:T(8,128)(2,1)S(1)} %copy-done, ...), custom_call_target="tpu_custom_call" | custom-call | flops 7549747200 | bytes 3010560 | tf_op jit(solution)/shard_map/tiles/pallas_call | solution.py:123
  48.7 10.1 %tiles.5 = (bf16[2,256,384]{2,1,0:T(8,128)(2,1)S(1)}, bf16[2,256,384]{2,1,0:T(8,128)(2,1)S(1)}, f32[2,384,256]{2,1,0:T(8,128)S(1)}, f32[2,384,256]{2,1,0:T(8,128)S(1)}, f32[2,384,256]{2,1,0:T(8,128)S(1)}) custom-call(bf16[2,1584,128]{2,1,0:T(8,128)(2,1)S(1)} %collective-permute-done.8.refs_0_, bf16[2,1584,128]{2,1,0:T(8,128)(2,1)S(1)} %collective-permute-done.9.refs_1_, ...), custom_call_target="tpu_custom_call" | custom-call | flops 9059696640 | bytes 2408448 | tf_op jit(solution)/shard_map/tiles/pallas_call | solution.py:123
  59.0 8.1 %collective-permute-start.15 = (bf16[2,384,256]{2,1,0:T(8,128)(2,1)S(1)}, bf16[2,384,256]{2,1,0:T(8,128)(2,1)S(1)}, u32[]{:S(2)}, u32[]{:S(2)}) collective-permute-start(bf16[2,384,256]{2,1,0:T(8,128)(2,1)S(1)} %convert_element_type.82), channel_id=1, source_target_pairs={{1,2},{2,1},{3,4},{4,3},{5,6},{6,5},{9,10},{10,9},{11,12},{12,11},... | collective-permute-start | bytes 1179656 | tf_op jit(solution)/shard_map/ppermute | solution.py:26
  67.3 2.4 %collective-permute-start.7 = (bf16[1,256,384]{2,1,0:T(8,128)(2,1)S(1)}, bf16[1,256,384]{2,1,0:T(8,128)(2,1)S(1)}, u32[]{:S(2)}, u32[]{:S(2)}) collective-permute-start(bf16[1,256,384]{2,1,0:T(8,128)(2,1)S(1)} %get-tuple-element.32), channel_id=1, source_target_pairs={{32,64},{64,32},{96,128},{128,96},{160,192},{192,160},{33,65},{65,... | collective-permute-start | bytes 589832 | tf_op jit(solution)/shard_map/ppermute | solution.py:26
  69.7 3.1 %collective-permute-start.10 = (bf16[2,256,384]{2,1,0:T(8,128)(2,1)S(1)}, bf16[2,256,384]{2,1,0:T(8,128)(2,1)S(1)}, u32[]{:S(2)}, u32[]{:S(2)}) collective-permute-start(bf16[2,256,384]{2,1,0:T(8,128)(2,1)S(1)} %get-tuple-element.37), channel_id=1, source_target_pairs={{32,64},{64,32},{96,128},{128,96},{160,192},{192,160},{33,65},{65,... | collective-permute-start | bytes 1179656 | tf_op jit(solution)/shard_map/ppermute | solution.py:26
  72.8 0.6 collective-permute-start.11
  73.4 5.3 %collective-permute-done.15 = bf16[2,384,256]{2,1,0:T(8,128)(2,1)S(1)} collective-permute-done((bf16[2,384,256]{2,1,0:T(8,128)(2,1)S(1)}, bf16[2,384,256]{2,1,0:T(8,128)(2,1)S(1)}, u32[]{:S(2)}, u32[]{:S(2)}) %collective-permute-start.15) | collective-permute-done | bytes 393248 | tf_op jit(solution)/shard_map/ppermute | solution.py:26
  78.8 0.7 fusion.4
  79.8 2.7 %collective-permute-start.13 = (bf16[1,256,384]{2,1,0:T(8,128)(2,1)S(1)}, bf16[1,256,384]{2,1,0:T(8,128)(2,1)S(1)}, u32[]{:S(2)}, u32[]{:S(2)}) collective-permute-start(bf16[1,256,384]{2,1,0:T(8,128)(2,1)S(1)} %get-tuple-element.47), channel_id=1, source_target_pairs={{8,16},{16,8},{9,17},{17,9},{10,18},{18,10},{11,19},{19,11},{12,20... | collective-permute-start | bytes 589832 | tf_op jit(solution)/shard_map/ppermute | solution.py:26
  82.5 0.7 fusion.5
  83.2 3.9 %collective-permute-done.12 = bf16[1,256,384]{2,1,0:T(8,128)(2,1)S(1)} collective-permute-done((bf16[1,256,384]{2,1,0:T(8,128)(2,1)S(1)}, bf16[1,256,384]{2,1,0:T(8,128)(2,1)S(1)}, u32[]{:S(2)}, u32[]{:S(2)}) %collective-permute-start.12) | collective-permute-done | bytes 196640 | tf_op jit(solution)/shard_map/ppermute | solution.py:26
  87.0 1.9 %collective-permute-done.13 = bf16[1,256,384]{2,1,0:T(8,128)(2,1)S(1)} collective-permute-done((bf16[1,256,384]{2,1,0:T(8,128)(2,1)S(1)}, bf16[1,256,384]{2,1,0:T(8,128)(2,1)S(1)}, u32[]{:S(2)}, u32[]{:S(2)}) %collective-permute-start.13) | collective-permute-done | bytes 196640 | tf_op jit(solution)/shard_map/ppermute | solution.py:26
  89.0 0.1 fusion.3
  89.1 0.8 copy.9
  (27 shorter events, 0.9 us)
Async XLA Ops:
  3.0 11.3 %collective-permute-start = (bf16[1,1584,128]{2,1,0:T(8,128)(2,1)}, bf16[1,1584,128]{2,1,0:T(8,128)(2,1)S(1)}, u32[]{:S(2)}, u32[]{:S(2)}) collective-permute-start(bf16[1,1584,128]{2,1,0:T(8,128)(2,1)} %get-tuple-element.23.refs_0_), channel_id=1, source_target_pairs={{0,8},{8,0},{16,24},{24,16},{1,9},{9,1},{17,25},{25,17},{2,10},{10... | collective-permute-start | bytes 1216520 | tf_op jit(solution)/shard_map/ppermute | solution.py:26
  3.1 19.4 %collective-permute-start.1 = (bf16[1,1584,128]{2,1,0:T(8,128)(2,1)}, bf16[1,1584,128]{2,1,0:T(8,128)(2,1)S(1)}, u32[]{:S(2)}, u32[]{:S(2)}) collective-permute-start(bf16[1,1584,128]{2,1,0:T(8,128)(2,1)} %get-tuple-element.23.refs_0_), channel_id=1, source_target_pairs={{8,16},{16,8},{9,17},{17,9},{10,18},{18,10},{11,19},{19,11},{12,20... | collective-permute-start | bytes 1216520 | tf_op jit(solution)/shard_map/ppermute | solution.py:26
  8.8 13.9 %collective-permute-start.2 = (bf16[1,1584,128]{2,1,0:T(8,128)(2,1)}, bf16[1,1584,128]{2,1,0:T(8,128)(2,1)S(1)}, u32[]{:S(2)}, u32[]{:S(2)}) collective-permute-start(bf16[1,1584,128]{2,1,0:T(8,128)(2,1)} %get-tuple-element.23.refs_0_), channel_id=1, source_target_pairs={{0,32},{32,0},{64,96},{96,64},{128,160},{160,128},{192,224},{224,1... | collective-permute-start | bytes 1216520 | tf_op jit(solution)/shard_map/ppermute | solution.py:26
  8.9 16.5 %collective-permute-start.3 = (bf16[1,1584,128]{2,1,0:T(8,128)(2,1)}, bf16[1,1584,128]{2,1,0:T(8,128)(2,1)S(1)}, u32[]{:S(2)}, u32[]{:S(2)}) collective-permute-start(bf16[1,1584,128]{2,1,0:T(8,128)(2,1)} %get-tuple-element.23.refs_0_), channel_id=1, source_target_pairs={{32,64},{64,32},{96,128},{128,96},{160,192},{192,160},{33,65},{65,... | collective-permute-start | bytes 1216520 | tf_op jit(solution)/shard_map/ppermute | solution.py:26
  11.3 18.0 %collective-permute-start.4 = (bf16[2,384,256]{2,1,0:T(8,128)(2,1)}, bf16[2,384,256]{2,1,0:T(8,128)(2,1)S(1)}, u32[]{:S(2)}, u32[]{:S(2)}) collective-permute-start(bf16[2,384,256]{2,1,0:T(8,128)(2,1)} %get-tuple-element.24.refs_5_.refs_2_), channel_id=1, source_target_pairs={{0,1},{1,0},{2,3},{3,2},{4,5},{5,4},{6,7},{7,6},{8,9},{9,8},{10,11... | collective-permute-start | bytes 1179656 | tf_op jit(solution)/shard_map/ppermute | solution.py:26
  14.3 26.5 %collective-permute-start.5 = (bf16[2,384,256]{2,1,0:T(8,128)(2,1)}, bf16[2,384,256]{2,1,0:T(8,128)(2,1)S(1)}, u32[]{:S(2)}, u32[]{:S(2)}) collective-permute-start(bf16[2,384,256]{2,1,0:T(8,128)(2,1)} %get-tuple-element.24.refs_5_.refs_2_), channel_id=1, source_target_pairs={{1,2},{2,1},{3,4},{4,3},{5,6},{6,5},{9,10},{10,9},{11,12},{12,11},... | collective-permute-start | bytes 1179656 | tf_op jit(solution)/shard_map/ppermute | solution.py:26
  22.5 2.8 %copy-start = (bf16[1,1584,128]{2,1,0:T(8,128)(2,1)S(1)}, bf16[1,1584,128]{2,1,0:T(8,128)(2,1)}, u32[]{:S(2)}) copy-start(bf16[1,1584,128]{2,1,0:T(8,128)(2,1)} %get-tuple-element.23.refs_0_) | copy-start | bytes 1216516
  22.5 2.8 %copy-start.1 = (bf16[2,384,256]{2,1,0:T(8,128)(2,1)S(1)}, bf16[2,384,256]{2,1,0:T(8,128)(2,1)}, u32[]{:S(2)}) copy-start(bf16[2,384,256]{2,1,0:T(8,128)(2,1)} %get-tuple-element.24.refs_5_.refs_2_) | copy-start | bytes 1179652
  22.6 26.1 %collective-permute-start.8 = (bf16[2,1584,128]{2,1,0:T(8,128)(2,1)S(1)}, bf16[2,1584,128]{2,1,0:T(8,128)(2,1)S(1)}, u32[]{:S(2)}, u32[]{:S(2)}) collective-permute-start(bf16[2,1584,128]{2,1,0:T(8,128)(2,1)S(1)} %constant_dynamic-update-slice_fusion), channel_id=1, source_target_pairs={{0,32},{32,0},{64,96},{96,64},{128,160},{160,128},{192,224},{224,1... | collective-permute-start | bytes 2433032 | tf_op jit(solution)/shard_map/ppermute | solution.py:26
  22.7 26.0 %collective-permute-start.9 = (bf16[2,1584,128]{2,1,0:T(8,128)(2,1)S(1)}, bf16[2,1584,128]{2,1,0:T(8,128)(2,1)S(1)}, u32[]{:S(2)}, u32[]{:S(2)}) collective-permute-start(bf16[2,1584,128]{2,1,0:T(8,128)(2,1)S(1)} %constant_dynamic-update-slice_fusion), channel_id=1, source_target_pairs={{32,64},{64,32},{96,128},{128,96},{160,192},{192,160},{33,65},{65,... | collective-permute-start | bytes 2433032 | tf_op jit(solution)/shard_map/ppermute | solution.py:26
  58.9 14.0 %collective-permute-start.14 = (bf16[2,384,256]{2,1,0:T(8,128)(2,1)S(1)}, bf16[2,384,256]{2,1,0:T(8,128)(2,1)S(1)}, u32[]{:S(2)}, u32[]{:S(2)}) collective-permute-start(bf16[2,384,256]{2,1,0:T(8,128)(2,1)S(1)} %convert_element_type.80), channel_id=1, source_target_pairs={{0,1},{1,0},{2,3},{3,2},{4,5},{5,4},{6,7},{7,6},{8,9},{9,8},{10,11... | collective-permute-start | bytes 1179656 | tf_op jit(solution)/shard_map/ppermute | solution.py:26
  59.0 19.7 %collective-permute-start.15 = (bf16[2,384,256]{2,1,0:T(8,128)(2,1)S(1)}, bf16[2,384,256]{2,1,0:T(8,128)(2,1)S(1)}, u32[]{:S(2)}, u32[]{:S(2)}) collective-permute-start(bf16[2,384,256]{2,1,0:T(8,128)(2,1)S(1)} %convert_element_type.82), channel_id=1, source_target_pairs={{1,2},{2,1},{3,4},{4,3},{5,6},{6,5},{9,10},{10,9},{11,12},{12,11},... | collective-permute-start | bytes 1179656 | tf_op jit(solution)/shard_map/ppermute | solution.py:26
  67.2 16.0 %collective-permute-start.6 = (bf16[1,256,384]{2,1,0:T(8,128)(2,1)S(1)}, bf16[1,256,384]{2,1,0:T(8,128)(2,1)S(1)}, u32[]{:S(2)}, u32[]{:S(2)}) collective-permute-start(bf16[1,256,384]{2,1,0:T(8,128)(2,1)S(1)} %get-tuple-element.31), channel_id=1, source_target_pairs={{0,32},{32,0},{64,96},{96,64},{128,160},{160,128},{192,224},{224,1... | collective-permute-start | bytes 589832 | tf_op jit(solution)/shard_map/ppermute | solution.py:26
  67.3 15.9 %collective-permute-start.7 = (bf16[1,256,384]{2,1,0:T(8,128)(2,1)S(1)}, bf16[1,256,384]{2,1,0:T(8,128)(2,1)S(1)}, u32[]{:S(2)}, u32[]{:S(2)}) collective-permute-start(bf16[1,256,384]{2,1,0:T(8,128)(2,1)S(1)} %get-tuple-element.32), channel_id=1, source_target_pairs={{32,64},{64,32},{96,128},{128,96},{160,192},{192,160},{33,65},{65,... | collective-permute-start | bytes 589832 | tf_op jit(solution)/shard_map/ppermute | solution.py:26
  69.7 9.8 %collective-permute-start.10 = (bf16[2,256,384]{2,1,0:T(8,128)(2,1)S(1)}, bf16[2,256,384]{2,1,0:T(8,128)(2,1)S(1)}, u32[]{:S(2)}, u32[]{:S(2)}) collective-permute-start(bf16[2,256,384]{2,1,0:T(8,128)(2,1)S(1)} %get-tuple-element.37), channel_id=1, source_target_pairs={{32,64},{64,32},{96,128},{128,96},{160,192},{192,160},{33,65},{65,... | collective-permute-start | bytes 1179656 | tf_op jit(solution)/shard_map/ppermute | solution.py:26
  72.8 6.7 %collective-permute-start.11 = (bf16[2,256,384]{2,1,0:T(8,128)(2,1)S(1)}, bf16[2,256,384]{2,1,0:T(8,128)(2,1)S(1)}, u32[]{:S(2)}, u32[]{:S(2)}) collective-permute-start(bf16[2,256,384]{2,1,0:T(8,128)(2,1)S(1)} %get-tuple-element.38), channel_id=1, source_target_pairs={{0,32},{32,0},{64,96},{96,64},{128,160},{160,128},{192,224},{224,1... | collective-permute-start | bytes 1179656 | tf_op jit(solution)/shard_map/ppermute | solution.py:26
  79.7 7.3 %collective-permute-start.12 = (bf16[1,256,384]{2,1,0:T(8,128)(2,1)S(1)}, bf16[1,256,384]{2,1,0:T(8,128)(2,1)S(1)}, u32[]{:S(2)}, u32[]{:S(2)}) collective-permute-start(bf16[1,256,384]{2,1,0:T(8,128)(2,1)S(1)} %get-tuple-element.46), channel_id=1, source_target_pairs={{0,8},{8,0},{16,24},{24,16},{1,9},{9,1},{17,25},{25,17},{2,10},{10... | collective-permute-start | bytes 589832 | tf_op jit(solution)/shard_map/ppermute | solution.py:26
  79.8 9.1 %collective-permute-start.13 = (bf16[1,256,384]{2,1,0:T(8,128)(2,1)S(1)}, bf16[1,256,384]{2,1,0:T(8,128)(2,1)S(1)}, u32[]{:S(2)}, u32[]{:S(2)}) collective-permute-start(bf16[1,256,384]{2,1,0:T(8,128)(2,1)S(1)} %get-tuple-element.47), channel_id=1, source_target_pairs={{8,16},{16,8},{9,17},{17,9},{10,18},{18,10},{11,19},{19,11},{12,20... | collective-permute-start | bytes 589832 | tf_op jit(solution)/shard_map/ppermute | solution.py:26

commit v3 on v2

v3 whole, which is shorter than its diff:
```python
import functools

import jax
import jax.numpy as jnp
from jax import lax
from jax.experimental import pallas as pl
from jax.experimental.pallas import tpu as pltpu
from jax.sharding import PartitionSpec as P

F32 = jnp.float32
BF16 = jnp.bfloat16
NT = (((1,), (1,)), ((), ()))
NN = (((1,), (0,)), ((), ()))
LANES = 128
VMEM_BYTES = 36 * 2**20


def dot(a, b, dims=NN):
    return lax.dot_general(a, b, dims, preferred_element_type=F32)


def meet(x, axis, second):
    pairs = []
    for i in range(second, lax.axis_size(axis) - 1, 2):
        pairs += [(i, i + 1), (i + 1, i)]
    return lax.ppermute(x, axis, pairs)


def payload_kernel(heads, q_ref, do_ref, o_ref, log_ref, k_ref, v_ref, pay_ref, kv_ref):
    rows = q_ref.shape[0]
    blocks = rows // LANES
    kv_ref[0] = k_ref[...]
    kv_ref[1] = v_ref[...]
    for h in range(heads):
        cols = slice(h * LANES, (h + 1) * LANES)
        pay_ref[0, h * rows:(h + 1) * rows, :] = q_ref[:, cols]
        pay_ref[0, (heads + h) * rows:(heads + h + 1) * rows, :] = do_ref[:, cols]
    products = do_ref[...].astype(F32) * o_ref[...].astype(F32)
    turned = products.T
    parts = []
    for h in range(heads):
        parts += [log_ref[h:h + 1, j * LANES:(j + 1) * LANES] for j in range(blocks)]
    for h in range(heads):
        delta = jnp.sum(turned[h * LANES:(h + 1) * LANES], axis=0, keepdims=True)
        parts += [delta[:, j * LANES:(j + 1) * LANES] for j in range(blocks)]
    parts.append(jnp.zeros((16 - len(parts), LANES), F32))
    rest = jnp.concatenate(parts, axis=0)
    at = 2 * heads * rows
    for piece in range(3):
        low = rest.astype(BF16)
        pay_ref[0, at + 16 * piece:at + 16 * (piece + 1), :] = low
        rest = rest - low.astype(F32)


def make_payloads(q, do, o, log_norm, k, v):
    rows, width = q.shape
    heads = log_norm.shape[0]
    return pl.pallas_call(
        functools.partial(payload_kernel, heads),
        out_shape=[
            jax.ShapeDtypeStruct((1, 2 * heads * rows + 48, LANES), BF16),
            jax.ShapeDtypeStruct((2, rows, width), BF16),
        ],
        compiler_params=pltpu.CompilerParams(vmem_limit_bytes=60 * 2**20),
        name="payloads",
    )(q, do, o, log_norm, k, v)


def tiles_kernel(sizes, sides, heads, scale, dq_sizes, more_acc, groups, *refs):
    pay_refs, refs = refs[:len(sizes)], refs[len(sizes):]
    kvs, refs = refs[:sides], refs[sides:]
    dq_in_refs, refs = refs[:len(dq_sizes)], refs[len(dq_sizes):]
    acc_ins, refs = (refs[:sides], refs[sides:]) if more_acc else (None, refs)
    dqs, accs = refs[:len(groups)], refs[len(groups):]
    pays = [(ref, i) for ref, n in zip(pay_refs, sizes) for i in range(n)]
    dq_ins = [(ref, i) for ref, n in zip(dq_in_refs, dq_sizes) for i in range(n)]
    rows = kvs[0].shape[1]
    blocks = rows // LANES

    def row_of(aux, kind):
        return jnp.concatenate([aux[kind * blocks + j:kind * blocks + j + 1] for j in range(blocks)], axis=1)

    at = 2 * heads * rows
    auxes = []
    for ref, i in pays:
        aux = ref[i, at:, :].astype(F32)
        auxes.append(aux[0:16] + aux[16:32] + aux[32:48])
    for h in range(heads):
        cols = slice(h * LANES, (h + 1) * LANES)
        q = jnp.concatenate([ref[i, h * rows:(h + 1) * rows, :] for ref, i in pays], axis=0)
        do = jnp.concatenate([ref[i, (heads + h) * rows:(heads + h + 1) * rows, :] for ref, i in pays], axis=0)
        log = jnp.concatenate([row_of(aux, h) for aux in auxes], axis=1)
        delta = jnp.concatenate([row_of(aux, heads + h) for aux in auxes], axis=1)
        dq = None
        for s in range(sides):
            k = kvs[s][0, :, cols]
            v = kvs[s][1, :, cols]
            p = jnp.exp(dot(k, q, NT) * scale - log)
            ds = (p * (dot(v, do, NT) - delta)).astype(BF16)
            dv = dot(p.astype(BF16), do)
            dk = dot(ds, q)
            if more_acc:
                dv = dv + acc_ins[s][1, :, cols]
                dk = dk + acc_ins[s][0, :, cols]
            accs[s][1, :, cols] = dv.astype(accs[s].dtype)
            accs[s][0, :, cols] = dk.astype(accs[s].dtype)
            part = dot(k.astype(F32).T.astype(BF16), ds)
            dq = part if dq is None else dq + part
        for out, group in zip(dqs, groups):
            for at_out, tile in enumerate(group):
                mine = dq[:, tile * rows:(tile + 1) * rows]
                if dq_ins:
                    ref, i = dq_ins[tile]
                    mine = mine + ref[i, cols, :]
                out[at_out, cols, :] = mine.astype(out.dtype)


def run_tiles(pays, kvs, heads, scale, groups, kinds, acc_kinds, dq_in=(), acc_in=(), weight=1):
    sizes = [pay.shape[0] for pay in pays]
    _, rows, width = kvs[0].shape
    here = pl.BlockSpec(memory_space=pltpu.VMEM)
    done = pl.pallas_call(
        functools.partial(
            tiles_kernel, sizes, len(kvs), heads, scale, [x.shape[0] for x in dq_in], bool(acc_in), groups
        ),
        in_specs=[here] * (len(pays) + len(kvs) + len(dq_in) + len(acc_in)),
        out_specs=[here] * (len(groups) + len(kvs)),
        out_shape=[jax.ShapeDtypeStruct((len(group), width, rows), kind) for group, kind in zip(groups, kinds)]
        + [jax.ShapeDtypeStruct((2, rows, width), kind) for kind in acc_kinds],
        compiler_params=pltpu.CompilerParams(vmem_limit_bytes=VMEM_BYTES),
        cost_estimate=pl.CostEstimate(
            flops=weight * 10 * sum(sizes) * len(kvs) * rows * rows * width, bytes_accessed=0, transcendentals=0
        ),
        name="tiles",
    )(*pays, *kvs, *dq_in, *acc_in)
    return done[:len(groups)], done[len(groups):]


def finish_kernel(scale, dq_ref, a_ref, b_ref, row_a_ref, row_b_ref, dkv_ref, dkv_a_ref, dkv_b_ref, q_out, k_out, v_out):
    dkv = [dkv_ref[i] + dkv_a_ref[i].astype(F32) + dkv_b_ref[i].astype(F32) for i in range(2)]
    k_out[...] = (dkv[0] * scale).astype(BF16)
    v_out[...] = dkv[1].astype(BF16)
    dq = dq_ref[0]
    for ref in (a_ref, b_ref, row_a_ref, row_b_ref):
        dq = dq + ref[0].astype(F32)
    q_out[...] = (dq * scale).T.astype(BF16)


def finish(dq, a, b, row_a, row_b, dkv, dkv_a, dkv_b, scale):
    _, rows, width = dkv.shape
    return pl.pallas_call(
        functools.partial(finish_kernel, scale),
        out_shape=[jax.ShapeDtypeStruct((rows, width), BF16)] * 3,
        compiler_params=pltpu.CompilerParams(vmem_limit_bytes=VMEM_BYTES),
        name="finish",
    )(dq, a, b, row_a, row_b, dkv, dkv_a, dkv_b)


def local(queries, key_vectors, value_vectors, forward_out, cotangent, log_norm):
    rows, width = queries.shape[3:]
    heads = log_norm.shape[3]
    scale = (width // heads) ** (-0.5)
    flat = (rows, width)
    own, own_kv = make_payloads(
        queries.reshape(flat),
        cotangent.reshape(flat),
        forward_out.reshape(flat),
        log_norm.reshape(heads, rows),
        key_vectors.reshape(flat),
        value_vectors.reshape(flat),
    )

    kv_b = meet(own_kv, "col", 1)
    kv_a = meet(own_kv, "col", 0)
    row_b = meet(own, "row", 1)
    row_a = meet(own, "row", 0)
    frame_b = meet(own, "frame", 1)
    frame_a = meet(own, "frame", 0)
    pair = jnp.concatenate([row_a, row_b], axis=0)
    pair_b = meet(pair, "frame", 1)
    pair_a = meet(pair, "frame", 0)

    work = functools.partial(run_tiles, heads=heads, scale=scale)
    near = [own, row_a, row_b, frame_a, frame_b]
    far = [pair_a, pair_b]
    near_dqs, accs = work(
        near, [own_kv, kv_a], groups=[[0], [1], [2], [3], [4]], kinds=[F32] * 5, acc_kinds=[F32] * 2, weight=3
    )
    far_dqs, (dkv, to_a) = work(
        far, [own_kv, kv_a], acc_in=accs, groups=[[0, 1], [2, 3]], kinds=[F32] * 2, acc_kinds=[F32, BF16], weight=0
    )
    (dq_own, dq_row_a, dq_row_b, dq_frame_a, dq_frame_b), (to_b,) = work(
        near + far,
        [kv_b],
        dq_in=[*near_dqs, *far_dqs],
        groups=[[0], [1], [2], [3, 5, 6], [4, 7, 8]],
        kinds=[F32] * 3 + [BF16] * 2,
        acc_kinds=[BF16],
        weight=0,
    )

    dkv_b = meet(to_b, "col", 1)
    dkv_a = meet(to_a, "col", 0)
    back_b = meet(dq_frame_b, "frame", 1)
    back_a = meet(dq_frame_a, "frame", 0)
    back = back_b.astype(F32) + back_a.astype(F32)
    row_back_b = meet((dq_row_b + back[2:3]).astype(BF16), "row", 1)
    row_back_a = meet((dq_row_a + back[1:2]).astype(BF16), "row", 0)
    grads = finish(dq_own, back_a, back_b, row_back_a, row_back_b, dkv, dkv_a, dkv_b, scale)
    return tuple(grad.reshape(queries.shape) for grad in grads)


def solution(mesh):
    placed = P("frame", "row", "col", None, None)
    return jax.shard_map(
        local,
        mesh=mesh,
        in_specs=(placed,) * 6,
        out_specs=(placed,) * 3,
        check_vma=False,
    )
```

time: 90.2 us -> 81 us (0.90)
  the two profiles are of different devices: /device:TPU:46 before, /device:TPU:15 now
where the time goes in v3:
time: 81 us; the launch traced here: 80.7 us
  starting transfers between devices  39.2 us (48%)
  Pallas kernels  24.5 us (30%)
  waiting for transfers between devices  15.9 us (20%)
    ppermute x14, starting transfers between devices, meet(): return lax.ppermute(x, axis, pairs)  39.2 us
    pallas_call x3, Pallas kernels, run_tiles(): pl.pallas_call(functools.partial(tiles_kernel, sizes, len(kvs), heads, sc...  21.1 us
    ppermute x14, waiting for transfers between devices, meet(): return lax.ppermute(x, axis, pairs)  15.9 us
    pallas_call x1, Pallas kernels, make_payloads(): pl.pallas_call(functools.partial(payload_kernel, heads), out_shape=[jax.S...  2.37 us
  transfers between devices with their start and end apart: 14, of which 4 were waited for; matrix products, arithmetic and copies ran while one was open for 0% of the time, Pallas kernels for 17%

profile of v3, /device:TPU:15, one launch (start us, length us, event | category | flops | bytes accessed | tf_op | source)
XLA Modules:
  0.0 80.7 jit_solution(11998912484676360712)
XLA Ops:
  0.6 2.4 %payloads.1 = (bf16[1,1584,128]{2,1,0:T(8,128)(2,1)}, bf16[2,384,256]{2,1,0:T(8,128)(2,1)}) custom-call(bf16[384,256]{1,0:T(8,128)(2,1)} %bitcast.9, bf16[384,256]{1,0:T(8,128)(2,1)} %bitcast.10, bf16[384,256]{1,0:T(8,128)(2,1)} %bitcast.11, f32[2,384]{1,0:T(2,128)} %bitcast.14, bf16[384,256]{1,0:T(8,128)(2,1)} %bitcast.12, bf16[384,256]{1,0:T(8,128)(2,1)} %bitcast.13), custom_call_target="tpu_custom_call" | custom-call | tf_op jit(solution)/shard_map/payloads/pallas_call | solution.py:58
  3.0 1.7 %collective-permute-start = (bf16[1,1584,128]{2,1,0:T(8,128)(2,1)}, bf16[1,1584,128]{2,1,0:T(8,128)(2,1)S(1)}, u32[]{:S(2)}, u32[]{:S(2)}) collective-permute-start(bf16[1,1584,128]{2,1,0:T(8,128)(2,1)} %get-tuple-element.25.refs_0_), channel_id=1, source_target_pairs={{0,8},{8,0},{16,24},{24,16},{1,9},{9,1},{17,25},{25,17},{2,10},{10... | collective-permute-start | bytes 1216520 | tf_op jit(solution)/shard_map/ppermute | solution.py:26
  4.7 0.7 collective-permute-start.1
  5.4 0.6 collective-permute-start.7
  6.0 8.5 %collective-permute-start.6 = (bf16[2,384,256]{2,1,0:T(8,128)(2,1)}, bf16[2,384,256]{2,1,0:T(8,128)(2,1)S(1)}, u32[]{:S(2)}, u32[]{:S(2)}) collective-permute-start(bf16[2,384,256]{2,1,0:T(8,128)(2,1)} %get-tuple-element.26.refs_5_.refs_2_), channel_id=1, source_target_pairs={{1,2},{2,1},{3,4},{4,3},{5,6},{6,5},{9,10},{10,9},{11,12},{12,11},... | collective-permute-start | bytes 1179656 | tf_op jit(solution)/shard_map/ppermute | solution.py:26
  14.5 4.6 %collective-permute-start.3 = (bf16[1,1584,128]{2,1,0:T(8,128)(2,1)}, bf16[1,1584,128]{2,1,0:T(8,128)(2,1)S(1)}, u32[]{:S(2)}, u32[]{:S(2)}) collective-permute-start(bf16[1,1584,128]{2,1,0:T(8,128)(2,1)} %get-tuple-element.25.refs_0_), channel_id=1, source_target_pairs={{32,64},{64,32},{96,128},{128,96},{160,192},{192,160},{33,65},{65,... | collective-permute-start | bytes 1216520 | tf_op jit(solution)/shard_map/ppermute | solution.py:26
  19.4 3.3 %collective-permute-start.5 = (bf16[2,1584,128]{2,1,0:T(8,128)(2,1)S(1)}, bf16[2,1584,128]{2,1,0:T(8,128)(2,1)S(1)}, u32[]{:S(2)}, u32[]{:S(2)}) collective-permute-start(bf16[2,1584,128]{2,1,0:T(8,128)(2,1)S(1)} %constant_dynamic-update-slice_fusion), channel_id=1, source_target_pairs={{32,64},{64,32},{96,128},{128,96},{160,192},{192,160},{33,65},{65,... | collective-permute-start | bytes 2433032 | tf_op jit(solution)/shard_map/ppermute | solution.py:26
  22.7 0.3 collective-permute-start.4
  23.0 2.3 %collective-permute-done.3.refs_4_ = bf16[1,1584,128]{2,1,0:T(8,128)(2,1)S(1)} collective-permute-done((bf16[1,1584,128]{2,1,0:T(8,128)(2,1)}, bf16[1,1584,128]{2,1,0:T(8,128)(2,1)S(1)}, u32[]{:S(2)}, u32[]{:S(2)}) %collective-permute-start.3) | collective-permute-done | bytes 405536 | tf_op jit(solution)/shard_map/ppermute | solution.py:26
  25.2 7.8 %tiles.3 = (f32[1,256,384]{2,1,0:T(8,128)S(1)}, f32[1,256,384]{2,1,0:T(8,128)S(1)}, f32[1,256,384]{2,1,0:T(8,128)S(1)}, f32[1,256,384]{2,1,0:T(8,128)S(1)}, f32[...) custom-call(bf16[1,1584,128]{2,1,0:T(8,128)(2,1)S(1)} %copy-done, ...), custom_call_target="tpu_custom_call" | custom-call | flops 11324620800 | tf_op jit(solution)/shard_map/tiles/pallas_call | solution.py:122
  33.0 0.8 collective-permute-done.5.refs_1_.refs_6_
  33.8 6.4 %tiles.4 = (f32[2,256,384]{2,1,0:T(8,128)S(1)}, f32[2,256,384]{2,1,0:T(8,128)S(1)}, f32[2,384,256]{2,1,0:T(8,128)S(1)}, bf16[2,384,256]{2,1,0:T(8,128)(2,1)S(1)}) custom-call(bf16[2,1584,128]{2,1,0:T(8,128)(2,1)S(1)} %collective-permute-done.4.refs_0_.refs_5_, bf16[2,1584,128]{2,1,0:T(8,128)(2,1)S(1)} %collective-permute-done.5.refs_1_.refs_6_, ...), custom_call_target="tpu_custom_call" | custom-call | tf_op jit(solution)/shard_map/tiles/pallas_call | solution.py:122
  40.2 6.9 %tiles.5 = (f32[1,256,384]{2,1,0:T(8,128)S(1)}, f32[1,256,384]{2,1,0:T(8,128)S(1)}, f32[1,256,384]{2,1,0:T(8,128)S(1)}, bf16[3,256,384]{2,1,0:T(8,128)(2,1)S(1)}...) custom-call(bf16[1,1584,128]{2,1,0:T(8,128)(2,1)S(1)} %copy-done, ...), custom_call_target="tpu_custom_call" | custom-call | tf_op jit(solution)/shard_map/tiles/pallas_call | solution.py:122
  47.1 0.5 collective-permute-start.8
  47.6 3.1 %collective-permute-start.9 = (bf16[3,256,384]{2,1,0:T(8,128)(2,1)S(1)}, bf16[3,256,384]{2,1,0:T(8,128)(2,1)S(1)}, u32[]{:S(2)}, u32[]{:S(2)}) collective-permute-start(bf16[3,256,384]{2,1,0:T(8,128)(2,1)S(1)} %get-tuple-element.38), channel_id=1, source_target_pairs={{32,64},{64,32},{96,128},{128,96},{160,192},{192,160},{33,65},{65,... | collective-permute-start | bytes 1769480 | tf_op jit(solution)/shard_map/ppermute | solution.py:26
  50.7 4.3 %collective-permute-start.13 = (bf16[2,384,256]{2,1,0:T(8,128)(2,1)S(1)}, bf16[2,384,256]{2,1,0:T(8,128)(2,1)S(1)}, u32[]{:S(2)}, u32[]{:S(2)}) collective-permute-start(bf16[2,384,256]{2,1,0:T(8,128)(2,1)S(1)} %get-tuple-element.43), channel_id=1, source_target_pairs={{1,2},{2,1},{3,4},{4,3},{5,6},{6,5},{9,10},{10,9},{11,12},{12,11},... | collective-permute-start | bytes 1179656 | tf_op jit(solution)/shard_map/ppermute | solution.py:26
  55.0 0.1 collective-permute-start.12
  55.1 3.9 %collective-permute-done.9.b_ref = bf16[3,256,384]{2,1,0:T(8,128)(2,1)S(1)} collective-permute-done((bf16[3,256,384]{2,1,0:T(8,128)(2,1)S(1)}, bf16[3,256,384]{2,1,0:T(8,128)(2,1)S(1)}, u32[]{:S(2)}, u32[]{:S(2)}) %collective-permute-start.9) | collective-permute-done | bytes 589856 | tf_op jit(solution)/shard_map/ppermute | solution.py:26
  59.1 0.1 convert_add_fusion
  59.2 0.1 fusion
  59.3 0.7 collective-permute-start.11
  60.0 10.8 %collective-permute-start.10 = (bf16[1,256,384]{2,1,0:T(8,128)(2,1)S(1)}, bf16[1,256,384]{2,1,0:T(8,128)(2,1)S(1)}, u32[]{:S(2)}, u32[]{:S(2)}) collective-permute-start(bf16[1,256,384]{2,1,0:T(8,128)(2,1)S(1)} %get-tuple-element.48), channel_id=1, source_target_pairs={{0,8},{8,0},{16,24},{24,16},{1,9},{9,1},{17,25},{25,17},{2,10},{10... | collective-permute-start | bytes 589832 | tf_op jit(solution)/shard_map/ppermute | solution.py:26
  70.8 8.9 %collective-permute-done.10.row_a_ref = bf16[1,256,384]{2,1,0:T(8,128)(2,1)S(1)} collective-permute-done((bf16[1,256,384]{2,1,0:T(8,128)(2,1)S(1)}, bf16[1,256,384]{2,1,0:T(8,128)(2,1)S(1)}, u32[]{:S(2)}, u32[]{:S(2)}) %collective-permute-start.10) | collective-permute-done | bytes 196640 | tf_op jit(solution)/shard_map/ppermute | solution.py:26
  79.7 1.1 %finish.1 = (bf16[384,256]{1,0:T(8,128)(2,1)}, bf16[384,256]{1,0:T(8,128)(2,1)}, bf16[384,256]{1,0:T(8,128)(2,1)}) custom-call(f32[1,256,384]{2,1,0:T(8,128)S(1)} %get-tuple-element.36.dq_ref, bf16[3,256,384]{2,1,0:T(8,128)(2,1)S(1)} %collective-permute-done.8.a_ref, bf16[3,256,384]{2,1,0:T(8,128)(2,1)S(1)} %collective-permute-done.9.b_ref, ...), custom_call_target="tpu_custom_call" | custom-call | tf_op jit(solution)/shard_map/finish/pallas_call | solution.py:151
  (17 shorter events, 0.2 us)
Async XLA Ops:
  3.0 22.2 %copy-start = (bf16[1,1584,128]{2,1,0:T(8,128)(2,1)S(1)}, bf16[1,1584,128]{2,1,0:T(8,128)(2,1)}, u32[]{:S(2)}) copy-start(bf16[1,1584,128]{2,1,0:T(8,128)(2,1)} %get-tuple-element.25.refs_0_) | copy-start | bytes 1216516
  3.0 22.2 %copy-start.1 = (bf16[2,384,256]{2,1,0:T(8,128)(2,1)S(1)}, bf16[2,384,256]{2,1,0:T(8,128)(2,1)}, u32[]{:S(2)}) copy-start(bf16[2,384,256]{2,1,0:T(8,128)(2,1)} %get-tuple-element.26.refs_5_.refs_2_) | copy-start | bytes 1179652
  3.0 16.1 %collective-permute-start = (bf16[1,1584,128]{2,1,0:T(8,128)(2,1)}, bf16[1,1584,128]{2,1,0:T(8,128)(2,1)S(1)}, u32[]{:S(2)}, u32[]{:S(2)}) collective-permute-start(bf16[1,1584,128]{2,1,0:T(8,128)(2,1)} %get-tuple-element.25.refs_0_), channel_id=1, source_target_pairs={{0,8},{8,0},{16,24},{24,16},{1,9},{9,1},{17,25},{25,17},{2,10},{10... | collective-permute-start | bytes 1216520 | tf_op jit(solution)/shard_map/ppermute | solution.py:26
  4.7 14.6 %collective-permute-start.1 = (bf16[1,1584,128]{2,1,0:T(8,128)(2,1)}, bf16[1,1584,128]{2,1,0:T(8,128)(2,1)S(1)}, u32[]{:S(2)}, u32[]{:S(2)}) collective-permute-start(bf16[1,1584,128]{2,1,0:T(8,128)(2,1)} %get-tuple-element.25.refs_0_), channel_id=1, source_target_pairs={{8,16},{16,8},{9,17},{17,9},{10,18},{18,10},{11,19},{19,11},{12,20... | collective-permute-start | bytes 1216520 | tf_op jit(solution)/shard_map/ppermute | solution.py:26
  5.4 17.3 %collective-permute-start.7 = (bf16[2,384,256]{2,1,0:T(8,128)(2,1)}, bf16[2,384,256]{2,1,0:T(8,128)(2,1)S(1)}, u32[]{:S(2)}, u32[]{:S(2)}) collective-permute-start(bf16[2,384,256]{2,1,0:T(8,128)(2,1)} %get-tuple-element.26.refs_5_.refs_2_), channel_id=1, source_target_pairs={{0,1},{1,0},{2,3},{3,2},{4,5},{5,4},{6,7},{7,6},{8,9},{9,8},{10,11... | collective-permute-start | bytes 1179656 | tf_op jit(solution)/shard_map/ppermute | solution.py:26
  6.0 34.1 %collective-permute-start.6 = (bf16[2,384,256]{2,1,0:T(8,128)(2,1)}, bf16[2,384,256]{2,1,0:T(8,128)(2,1)S(1)}, u32[]{:S(2)}, u32[]{:S(2)}) collective-permute-start(bf16[2,384,256]{2,1,0:T(8,128)(2,1)} %get-tuple-element.26.refs_5_.refs_2_), channel_id=1, source_target_pairs={{1,2},{2,1},{3,4},{4,3},{5,6},{6,5},{9,10},{10,9},{11,12},{12,11},... | collective-permute-start | bytes 1179656 | tf_op jit(solution)/shard_map/ppermute | solution.py:26
  14.5 10.7 %collective-permute-start.3 = (bf16[1,1584,128]{2,1,0:T(8,128)(2,1)}, bf16[1,1584,128]{2,1,0:T(8,128)(2,1)S(1)}, u32[]{:S(2)}, u32[]{:S(2)}) collective-permute-start(bf16[1,1584,128]{2,1,0:T(8,128)(2,1)} %get-tuple-element.25.refs_0_), channel_id=1, source_target_pairs={{32,64},{64,32},{96,128},{128,96},{160,192},{192,160},{33,65},{65,... | collective-permute-start | bytes 1216520 | tf_op jit(solution)/shard_map/ppermute | solution.py:26
  19.2 6.1 %collective-permute-start.2 = (bf16[1,1584,128]{2,1,0:T(8,128)(2,1)}, bf16[1,1584,128]{2,1,0:T(8,128)(2,1)S(1)}, u32[]{:S(2)}, u32[]{:S(2)}) collective-permute-start(bf16[1,1584,128]{2,1,0:T(8,128)(2,1)} %get-tuple-element.25.refs_0_), channel_id=1, source_target_pairs={{0,32},{32,0},{64,96},{96,64},{128,160},{160,128},{192,224},{224,1... | collective-permute-start | bytes 1216520 | tf_op jit(solution)/shard_map/ppermute | solution.py:26
  19.4 14.4 %collective-permute-start.5 = (bf16[2,1584,128]{2,1,0:T(8,128)(2,1)S(1)}, bf16[2,1584,128]{2,1,0:T(8,128)(2,1)S(1)}, u32[]{:S(2)}, u32[]{:S(2)}) collective-permute-start(bf16[2,1584,128]{2,1,0:T(8,128)(2,1)S(1)} %constant_dynamic-update-slice_fusion), channel_id=1, source_target_pairs={{32,64},{64,32},{96,128},{128,96},{160,192},{192,160},{33,65},{65,... | collective-permute-start | bytes 2433032 | tf_op jit(solution)/shard_map/ppermute | solution.py:26
  22.7 11.1 %collective-permute-start.4 = (bf16[2,1584,128]{2,1,0:T(8,128)(2,1)S(1)}, bf16[2,1584,128]{2,1,0:T(8,128)(2,1)S(1)}, u32[]{:S(2)}, u32[]{:S(2)}) collective-permute-start(bf16[2,1584,128]{2,1,0:T(8,128)(2,1)S(1)} %constant_dynamic-update-slice_fusion), channel_id=1, source_target_pairs={{0,32},{32,0},{64,96},{96,64},{128,160},{160,128},{192,224},{224,1... | collective-permute-start | bytes 2433032 | tf_op jit(solution)/shard_map/ppermute | solution.py:26
  47.1 8.0 %collective-permute-start.8 = (bf16[3,256,384]{2,1,0:T(8,128)(2,1)S(1)}, bf16[3,256,384]{2,1,0:T(8,128)(2,1)S(1)}, u32[]{:S(2)}, u32[]{:S(2)}) collective-permute-start(bf16[3,256,384]{2,1,0:T(8,128)(2,1)S(1)} %get-tuple-element.37), channel_id=1, source_target_pairs={{0,32},{32,0},{64,96},{96,64},{128,160},{160,128},{192,224},{224,1... | collective-permute-start | bytes 1769480 | tf_op jit(solution)/shard_map/ppermute | solution.py:26
  47.6 11.5 %collective-permute-start.9 = (bf16[3,256,384]{2,1,0:T(8,128)(2,1)S(1)}, bf16[3,256,384]{2,1,0:T(8,128)(2,1)S(1)}, u32[]{:S(2)}, u32[]{:S(2)}) collective-permute-start(bf16[3,256,384]{2,1,0:T(8,128)(2,1)S(1)} %get-tuple-element.38), channel_id=1, source_target_pairs={{32,64},{64,32},{96,128},{128,96},{160,192},{192,160},{33,65},{65,... | collective-permute-start | bytes 1769480 | tf_op jit(solution)/shard_map/ppermute | solution.py:26
  50.7 20.1 %collective-permute-start.13 = (bf16[2,384,256]{2,1,0:T(8,128)(2,1)S(1)}, bf16[2,384,256]{2,1,0:T(8,128)(2,1)S(1)}, u32[]{:S(2)}, u32[]{:S(2)}) collective-permute-start(bf16[2,384,256]{2,1,0:T(8,128)(2,1)S(1)} %get-tuple-element.43), channel_id=1, source_target_pairs={{1,2},{2,1},{3,4},{4,3},{5,6},{6,5},{9,10},{10,9},{11,12},{12,11},... | collective-permute-start | bytes 1179656 | tf_op jit(solution)/shard_map/ppermute | solution.py:26
  55.0 15.8 %collective-permute-start.12 = (bf16[2,384,256]{2,1,0:T(8,128)(2,1)S(1)}, bf16[2,384,256]{2,1,0:T(8,128)(2,1)S(1)}, u32[]{:S(2)}, u32[]{:S(2)}) collective-permute-start(bf16[2,384,256]{2,1,0:T(8,128)(2,1)S(1)} %get-tuple-element.42), channel_id=1, source_target_pairs={{0,1},{1,0},{2,3},{3,2},{4,5},{5,4},{6,7},{7,6},{8,9},{9,8},{10,11... | collective-permute-start | bytes 1179656 | tf_op jit(solution)/shard_map/ppermute | solution.py:26
  59.3 11.5 %collective-permute-start.11 = (bf16[1,256,384]{2,1,0:T(8,128)(2,1)S(1)}, bf16[1,256,384]{2,1,0:T(8,128)(2,1)S(1)}, u32[]{:S(2)}, u32[]{:S(2)}) collective-permute-start(bf16[1,256,384]{2,1,0:T(8,128)(2,1)S(1)} %get-tuple-element.47), channel_id=1, source_target_pairs={{8,16},{16,8},{9,17},{17,9},{10,18},{18,10},{11,19},{19,11},{12,20... | collective-permute-start | bytes 589832 | tf_op jit(solution)/shard_map/ppermute | solution.py:26
  60.0 19.7 %collective-permute-start.10 = (bf16[1,256,384]{2,1,0:T(8,128)(2,1)S(1)}, bf16[1,256,384]{2,1,0:T(8,128)(2,1)S(1)}, u32[]{:S(2)}, u32[]{:S(2)}) collective-permute-start(bf16[1,256,384]{2,1,0:T(8,128)(2,1)S(1)} %get-tuple-element.48), channel_id=1, source_target_pairs={{0,8},{8,0},{16,24},{24,16},{1,9},{9,1},{17,25},{25,17},{2,10},{10... | collective-permute-start | bytes 589832 | tf_op jit(solution)/shard_map/ppermute | solution.py:26

commit v4 on v3

--- a/solution.py
+++ b/solution.py
@@ -12,6 +12,8 @@
 NT = (((1,), (1,)), ((), ()))
 NN = (((1,), (0,)), ((), ()))
 LANES = 128
+CHUNK = 256
+LOG2_E = 1.4426950408889634
 VMEM_BYTES = 36 * 2**20
 
 
@@ -26,22 +28,33 @@
     return lax.ppermute(x, axis, pairs)
 
 
-def payload_kernel(heads, q_ref, do_ref, o_ref, log_ref, k_ref, v_ref, pay_ref, kv_ref):
+def payload_kernel(heads, q_ref, do_ref, o_ref, log_ref, k_ref, v_ref, pay_ref, kv_ref, o_buf, log_buf, sems):
     rows = q_ref.shape[0]
     blocks = rows // LANES
-    kv_ref[0] = k_ref[...]
-    kv_ref[1] = v_ref[...]
-    for h in range(heads):
-        cols = slice(h * LANES, (h + 1) * LANES)
-        pay_ref[0, h * rows:(h + 1) * rows, :] = q_ref[:, cols]
-        pay_ref[0, (heads + h) * rows:(heads + h + 1) * rows, :] = do_ref[:, cols]
-    products = do_ref[...].astype(F32) * o_ref[...].astype(F32)
-    turned = products.T
+    copies = []
+
+    def copy(src, dst):
+        copies.append(pltpu.make_async_copy(src, dst, sems.at[len(copies)]))
+        copies[-1].start()
+
+    for h in range(heads):
+        copy(do_ref.at[:, h * LANES:(h + 1) * LANES], pay_ref.at[0, (heads + h) * rows:(heads + h + 1) * rows, :])
+    copy(o_ref, o_buf)
+    copy(log_ref, log_buf)
+    needed = len(copies)
+    for h in range(heads):
+        copy(q_ref.at[:, h * LANES:(h + 1) * LANES], pay_ref.at[0, h * rows:(h + 1) * rows, :])
+    copy(k_ref, kv_ref.at[0])
+    copy(v_ref, kv_ref.at[1])
+    for one in copies[:needed]:
+        one.wait()
     parts = []
     for h in range(heads):
-        parts += [log_ref[h:h + 1, j * LANES:(j + 1) * LANES] for j in range(blocks)]
-    for h in range(heads):
-        delta = jnp.sum(turned[h * LANES:(h + 1) * LANES], axis=0, keepdims=True)
+        parts += [log_buf[h:h + 1, j * LANES:(j + 1) * LANES] for j in range(blocks)]
+    for h in range(heads):
+        do = pay_ref[0, (heads + h) * rows:(heads + h + 1) * rows, :].astype(F32)
+        products = do * o_buf[:, h * LANES:(h + 1) * LANES].astype(F32)
+        delta = jnp.sum(products.T, axis=0, keepdims=True)
         parts += [delta[:, j * LANES:(j + 1) * LANES] for j in range(blocks)]
     parts.append(jnp.zeros((16 - len(parts), LANES), F32))
     rest = jnp.concatenate(parts, axis=0)
@@ -50,6 +63,8 @@
         low = rest.astype(BF16)
         pay_ref[0, at + 16 * piece:at + 16 * (piece + 1), :] = low
         rest = rest - low.astype(F32)
+    for one in copies[needed:]:
+        one.wait()
 
 
 def make_payloads(q, do, o, log_norm, k, v):
@@ -57,9 +72,16 @@
     heads = log_norm.shape[0]
     return pl.pallas_call(
         functools.partial(payload_kernel, heads),
+        in_specs=[pl.BlockSpec(memory_space=pltpu.HBM)] * 6,
+        out_specs=[pl.BlockSpec(memory_space=pltpu.VMEM)] * 2,
         out_shape=[
             jax.ShapeDtypeStruct((1, 2 * heads * rows + 48, LANES), BF16),
             jax.ShapeDtypeStruct((2, rows, width), BF16),
+        ],
+        scratch_shapes=[
+            pltpu.VMEM((rows, width), BF16),
+            pltpu.VMEM(log_norm.shape, F32),
+            pltpu.SemaphoreType.DMA((2 * heads + 4,)),
         ],
         compiler_params=pltpu.CompilerParams(vmem_limit_bytes=60 * 2**20),
         name="payloads",
@@ -71,7 +93,8 @@
     kvs, refs = refs[:sides], refs[sides:]
     dq_in_refs, refs = refs[:len(dq_sizes)], refs[len(dq_sizes):]
     acc_ins, refs = (refs[:sides], refs[sides:]) if more_acc else (None, refs)
-    dqs, accs = refs[:len(groups)], refs[len(groups):]
+    dqs, refs = refs[:len(groups)], refs[len(groups):]
+    accs, (p_ref, ds_ref) = refs[:sides], refs[sides:]
     pays = [(ref, i) for ref, n in zip(pay_refs, sizes) for i in range(n)]
     dq_ins = [(ref, i) for ref, n in zip(dq_in_refs, dq_sizes) for i in range(n)]
     rows = kvs[0].shape[1]
@@ -91,13 +114,20 @@
         do = jnp.concatenate([ref[i, (heads + h) * rows:(heads + h + 1) * rows, :] for ref, i in pays], axis=0)
         log = jnp.concatenate([row_of(aux, h) for aux in auxes], axis=1)
         delta = jnp.concatenate([row_of(aux, heads + h) for aux in auxes], axis=1)
+        log = log * LOG2_E
         dq = None
         for s in range(sides):
             k = kvs[s][0, :, cols]
             v = kvs[s][1, :, cols]
-            p = jnp.exp(dot(k, q, NT) * scale - log)
-            ds = (p * (dot(v, do, NT) - delta)).astype(BF16)
-            dv = dot(p.astype(BF16), do)
+            for start in range(0, q.shape[0], CHUNK):
+                part = slice(start, min(start + CHUNK, q.shape[0]))
+                p = jnp.exp2(dot(k, q[part], NT) * (scale * LOG2_E) - log[:, part])
+                ds = p * (dot(v, do[part], NT) - delta[:, part])
+                p_ref[h * sides + s, :, part] = p.astype(BF16)
+                ds_ref[h * sides + s, :, part] = ds.astype(BF16)
+            p = p_ref[h * sides + s]
+            ds = ds_ref[h * sides + s]
+            dv = dot(p, do)
             dk = dot(ds, q)
             if more_acc:
                 dv = dv + acc_ins[s][1, :, cols]
@@ -127,6 +157,7 @@
         out_specs=[here] * (len(groups) + len(kvs)),
         out_shape=[jax.ShapeDtypeStruct((len(group), width, rows), kind) for group, kind in zip(groups, kinds)]
         + [jax.ShapeDtypeStruct((2, rows, width), kind) for kind in acc_kinds],
+        scratch_shapes=[pltpu.VMEM((heads * len(kvs), rows, sum(sizes) * rows), BF16)] * 2,
         compiler_params=pltpu.CompilerParams(vmem_limit_bytes=VMEM_BYTES),
         cost_estimate=pl.CostEstimate(
             flops=weight * 10 * sum(sizes) * len(kvs) * rows * rows * width, bytes_accessed=0, transcendentals=0

time: 81 us -> 80.6 us (level)
  no operation moved by 1% of the time
where the time goes in v4:
time: 80.6 us; the launch traced here: 80.3 us
  starting transfers between devices  39.2 us (49%)
  Pallas kernels  23.9 us (30%)
  waiting for transfers between devices  16.1 us (20%)
  between operations  0.83 us (1%)
    ppermute x14, starting transfers between devices, meet(): return lax.ppermute(x, axis, pairs)  39.2 us
    pallas_call x3, Pallas kernels, run_tiles(): pl.pallas_call(functools.partial(tiles_kernel, sizes, len(kvs), heads, sc...  20.6 us
    ppermute x14, waiting for transfers between devices, meet(): return lax.ppermute(x, axis, pairs)  16.1 us
    pallas_call x1, Pallas kernels, make_payloads(): pl.pallas_call(functools.partial(payload_kernel, heads), in_specs=[pl.Blo...  2.26 us
  transfers between devices with their start and end apart: 14, of which 4 were waited for; matrix products, arithmetic and copies ran while one was open for 0% of the time, Pallas kernels for 17%

profile of v4, /device:TPU:15, one launch (start us, length us, event | category | flops | bytes accessed | tf_op | source)
XLA Modules:
  0.0 80.3 jit_solution(4501540678563135551)
XLA Ops:
  0.6 2.3 %payloads.1 = (bf16[1,1584,128]{2,1,0:T(8,128)(2,1)}, bf16[2,384,256]{2,1,0:T(8,128)(2,1)}) custom-call(bf16[384,256]{1,0:T(8,128)(2,1)} %bitcast.9, bf16[384,256]{1,0:T(8,128)(2,1)} %bitcast.10, bf16[384,256]{1,0:T(8,128)(2,1)} %bitcast.11, f32[2,384]{1,0:T(2,128)} %bitcast.14, bf16[384,256]{1,0:T(8,128)(2,1)} %bitcast.12, bf16[384,256]{1,0:T(8,128)(2,1)} %bitcast.13), custom_call_target="tpu_custom_call" | custom-call | tf_op jit(solution)/shard_map/payloads/pallas_call | solution.py:73
  2.9 1.7 %collective-permute-start = (bf16[1,1584,128]{2,1,0:T(8,128)(2,1)}, bf16[1,1584,128]{2,1,0:T(8,128)(2,1)S(1)}, u32[]{:S(2)}, u32[]{:S(2)}) collective-permute-start(bf16[1,1584,128]{2,1,0:T(8,128)(2,1)} %get-tuple-element.25.refs_0_), channel_id=1, source_target_pairs={{0,8},{8,0},{16,24},{24,16},{1,9},{9,1},{17,25},{25,17},{2,10},{10... | collective-permute-start | bytes 1216520 | tf_op jit(solution)/shard_map/ppermute | solution.py:28
  4.6 0.7 collective-permute-start.1
  5.3 0.6 collective-permute-start.7
  6.0 8.5 %collective-permute-start.6 = (bf16[2,384,256]{2,1,0:T(8,128)(2,1)}, bf16[2,384,256]{2,1,0:T(8,128)(2,1)S(1)}, u32[]{:S(2)}, u32[]{:S(2)}) collective-permute-start(bf16[2,384,256]{2,1,0:T(8,128)(2,1)} %get-tuple-element.26.refs_5_.refs_2_), channel_id=1, source_target_pairs={{1,2},{2,1},{3,4},{4,3},{5,6},{6,5},{9,10},{10,9},{11,12},{12,11},... | collective-permute-start | bytes 1179656 | tf_op jit(solution)/shard_map/ppermute | solution.py:28
  14.5 4.6 %collective-permute-start.3 = (bf16[1,1584,128]{2,1,0:T(8,128)(2,1)}, bf16[1,1584,128]{2,1,0:T(8,128)(2,1)S(1)}, u32[]{:S(2)}, u32[]{:S(2)}) collective-permute-start(bf16[1,1584,128]{2,1,0:T(8,128)(2,1)} %get-tuple-element.25.refs_0_), channel_id=1, source_target_pairs={{32,64},{64,32},{96,128},{128,96},{160,192},{192,160},{33,65},{65,... | collective-permute-start | bytes 1216520 | tf_op jit(solution)/shard_map/ppermute | solution.py:28
  19.3 3.3 %collective-permute-start.5 = (bf16[2,1584,128]{2,1,0:T(8,128)(2,1)S(1)}, bf16[2,1584,128]{2,1,0:T(8,128)(2,1)S(1)}, u32[]{:S(2)}, u32[]{:S(2)}) collective-permute-start(bf16[2,1584,128]{2,1,0:T(8,128)(2,1)S(1)} %constant_dynamic-update-slice_fusion), channel_id=1, source_target_pairs={{32,64},{64,32},{96,128},{128,96},{160,192},{192,160},{33,65},{65,... | collective-permute-start | bytes 2433032 | tf_op jit(solution)/shard_map/ppermute | solution.py:28
  22.6 0.3 collective-permute-start.4
  22.9 2.3 %collective-permute-done.3.refs_4_ = bf16[1,1584,128]{2,1,0:T(8,128)(2,1)S(1)} collective-permute-done((bf16[1,1584,128]{2,1,0:T(8,128)(2,1)}, bf16[1,1584,128]{2,1,0:T(8,128)(2,1)S(1)}, u32[]{:S(2)}, u32[]{:S(2)}) %collective-permute-start.3) | collective-permute-done | bytes 405536 | tf_op jit(solution)/shard_map/ppermute | solution.py:28
  25.2 7.5 %tiles.3 = (f32[1,256,384]{2,1,0:T(8,128)S(1)}, f32[1,256,384]{2,1,0:T(8,128)S(1)}, f32[1,256,384]{2,1,0:T(8,128)S(1)}, f32[1,256,384]{2,1,0:T(8,128)S(1)}, f32[...) custom-call(bf16[1,1584,128]{2,1,0:T(8,128)(2,1)S(1)} %copy-done, ...), custom_call_target="tpu_custom_call" | custom-call | flops 11324620800 | tf_op jit(solution)/shard_map/tiles/pallas_call | solution.py:152
  32.7 1.0 %collective-permute-done.5.refs_1_.refs_6_ = bf16[2,1584,128]{2,1,0:T(8,128)(2,1)S(1)} collective-permute-done((bf16[2,1584,128]{2,1,0:T(8,128)(2,1)S(1)}, bf16[2,1584,128]{2,1,0:T(8,128)(2,1)S(1)}, u32[]{:S(2)}, u32[]{:S(2)}) %collective-permute-start.5) | collective-permute-done | bytes 811040 | tf_op jit(solution)/shard_map/ppermute | solution.py:28
  33.7 6.0 %tiles.4 = (f32[2,256,384]{2,1,0:T(8,128)S(1)}, f32[2,256,384]{2,1,0:T(8,128)S(1)}, f32[2,384,256]{2,1,0:T(8,128)S(1)}, bf16[2,384,256]{2,1,0:T(8,128)(2,1)S(1)}) custom-call(bf16[2,1584,128]{2,1,0:T(8,128)(2,1)S(1)} %collective-permute-done.4.refs_0_.refs_5_, bf16[2,1584,128]{2,1,0:T(8,128)(2,1)S(1)} %collective-permute-done.5.refs_1_.refs_6_, ...), custom_call_target="tpu_custom_call" | custom-call | tf_op jit(solution)/shard_map/tiles/pallas_call | solution.py:152
  39.7 7.1 %tiles.5 = (f32[1,256,384]{2,1,0:T(8,128)S(1)}, f32[1,256,384]{2,1,0:T(8,128)S(1)}, f32[1,256,384]{2,1,0:T(8,128)S(1)}, bf16[3,256,384]{2,1,0:T(8,128)(2,1)S(1)}...) custom-call(bf16[1,1584,128]{2,1,0:T(8,128)(2,1)S(1)} %copy-done, ...), custom_call_target="tpu_custom_call" | custom-call | tf_op jit(solution)/shard_map/tiles/pallas_call | solution.py:152
  46.7 0.5 collective-permute-start.8
  47.2 3.1 %collective-permute-start.9 = (bf16[3,256,384]{2,1,0:T(8,128)(2,1)S(1)}, bf16[3,256,384]{2,1,0:T(8,128)(2,1)S(1)}, u32[]{:S(2)}, u32[]{:S(2)}) collective-permute-start(bf16[3,256,384]{2,1,0:T(8,128)(2,1)S(1)} %get-tuple-element.38), channel_id=1, source_target_pairs={{32,64},{64,32},{96,128},{128,96},{160,192},{192,160},{33,65},{65,... | collective-permute-start | bytes 1769480 | tf_op jit(solution)/shard_map/ppermute | solution.py:28
  50.3 4.3 %collective-permute-start.13 = (bf16[2,384,256]{2,1,0:T(8,128)(2,1)S(1)}, bf16[2,384,256]{2,1,0:T(8,128)(2,1)S(1)}, u32[]{:S(2)}, u32[]{:S(2)}) collective-permute-start(bf16[2,384,256]{2,1,0:T(8,128)(2,1)S(1)} %get-tuple-element.43), channel_id=1, source_target_pairs={{1,2},{2,1},{3,4},{4,3},{5,6},{6,5},{9,10},{10,9},{11,12},{12,11},... | collective-permute-start | bytes 1179656 | tf_op jit(solution)/shard_map/ppermute | solution.py:28
  54.6 0.1 collective-permute-start.12
  54.8 4.0 %collective-permute-done.9.b_ref = bf16[3,256,384]{2,1,0:T(8,128)(2,1)S(1)} collective-permute-done((bf16[3,256,384]{2,1,0:T(8,128)(2,1)S(1)}, bf16[3,256,384]{2,1,0:T(8,128)(2,1)S(1)}, u32[]{:S(2)}, u32[]{:S(2)}) %collective-permute-start.9) | collective-permute-done | bytes 589856 | tf_op jit(solution)/shard_map/ppermute | solution.py:28
  58.7 0.1 convert_add_fusion
  58.8 0.1 fusion
  58.9 0.7 collective-permute-start.11
  59.6 10.8 %collective-permute-start.10 = (bf16[1,256,384]{2,1,0:T(8,128)(2,1)S(1)}, bf16[1,256,384]{2,1,0:T(8,128)(2,1)S(1)}, u32[]{:S(2)}, u32[]{:S(2)}) collective-permute-start(bf16[1,256,384]{2,1,0:T(8,128)(2,1)S(1)} %get-tuple-element.48), channel_id=1, source_target_pairs={{0,8},{8,0},{16,24},{24,16},{1,9},{9,1},{17,25},{25,17},{2,10},{10... | collective-permute-start | bytes 589832 | tf_op jit(solution)/shard_map/ppermute | solution.py:28
  70.4 8.9 %collective-permute-done.10.row_a_ref = bf16[1,256,384]{2,1,0:T(8,128)(2,1)S(1)} collective-permute-done((bf16[1,256,384]{2,1,0:T(8,128)(2,1)S(1)}, bf16[1,256,384]{2,1,0:T(8,128)(2,1)S(1)}, u32[]{:S(2)}, u32[]{:S(2)}) %collective-permute-start.10) | collective-permute-done | bytes 196640 | tf_op jit(solution)/shard_map/ppermute | solution.py:28
  79.3 1.1 %finish.1 = (bf16[384,256]{1,0:T(8,128)(2,1)}, bf16[384,256]{1,0:T(8,128)(2,1)}, bf16[384,256]{1,0:T(8,128)(2,1)}) custom-call(f32[1,256,384]{2,1,0:T(8,128)S(1)} %get-tuple-element.36.dq_ref, bf16[3,256,384]{2,1,0:T(8,128)(2,1)S(1)} %collective-permute-done.8.a_ref, bf16[3,256,384]{2,1,0:T(8,128)(2,1)S(1)} %collective-permute-done.9.b_ref, ...), custom_call_target="tpu_custom_call" | custom-call | tf_op jit(solution)/shard_map/finish/pallas_call | solution.py:182
  (17 shorter events, 0.2 us)
Async XLA Ops:
  2.9 22.3 %copy-start = (bf16[1,1584,128]{2,1,0:T(8,128)(2,1)S(1)}, bf16[1,1584,128]{2,1,0:T(8,128)(2,1)}, u32[]{:S(2)}) copy-start(bf16[1,1584,128]{2,1,0:T(8,128)(2,1)} %get-tuple-element.25.refs_0_) | copy-start | bytes 1216516
  2.9 22.2 %copy-start.1 = (bf16[2,384,256]{2,1,0:T(8,128)(2,1)S(1)}, bf16[2,384,256]{2,1,0:T(8,128)(2,1)}, u32[]{:S(2)}) copy-start(bf16[2,384,256]{2,1,0:T(8,128)(2,1)} %get-tuple-element.26.refs_5_.refs_2_) | copy-start | bytes 1179652
  2.9 16.1 %collective-permute-start = (bf16[1,1584,128]{2,1,0:T(8,128)(2,1)}, bf16[1,1584,128]{2,1,0:T(8,128)(2,1)S(1)}, u32[]{:S(2)}, u32[]{:S(2)}) collective-permute-start(bf16[1,1584,128]{2,1,0:T(8,128)(2,1)} %get-tuple-element.25.refs_0_), channel_id=1, source_target_pairs={{0,8},{8,0},{16,24},{24,16},{1,9},{9,1},{17,25},{25,17},{2,10},{10... | collective-permute-start | bytes 1216520 | tf_op jit(solution)/shard_map/ppermute | solution.py:28
  4.6 14.6 %collective-permute-start.1 = (bf16[1,1584,128]{2,1,0:T(8,128)(2,1)}, bf16[1,1584,128]{2,1,0:T(8,128)(2,1)S(1)}, u32[]{:S(2)}, u32[]{:S(2)}) collective-permute-start(bf16[1,1584,128]{2,1,0:T(8,128)(2,1)} %get-tuple-element.25.refs_0_), channel_id=1, source_target_pairs={{8,16},{16,8},{9,17},{17,9},{10,18},{18,10},{11,19},{19,11},{12,20... | collective-permute-start | bytes 1216520 | tf_op jit(solution)/shard_map/ppermute | solution.py:28
  5.3 17.3 %collective-permute-start.7 = (bf16[2,384,256]{2,1,0:T(8,128)(2,1)}, bf16[2,384,256]{2,1,0:T(8,128)(2,1)S(1)}, u32[]{:S(2)}, u32[]{:S(2)}) collective-permute-start(bf16[2,384,256]{2,1,0:T(8,128)(2,1)} %get-tuple-element.26.refs_5_.refs_2_), channel_id=1, source_target_pairs={{0,1},{1,0},{2,3},{3,2},{4,5},{5,4},{6,7},{7,6},{8,9},{9,8},{10,11... | collective-permute-start | bytes 1179656 | tf_op jit(solution)/shard_map/ppermute | solution.py:28
  6.0 33.7 %collective-permute-start.6 = (bf16[2,384,256]{2,1,0:T(8,128)(2,1)}, bf16[2,384,256]{2,1,0:T(8,128)(2,1)S(1)}, u32[]{:S(2)}, u32[]{:S(2)}) collective-permute-start(bf16[2,384,256]{2,1,0:T(8,128)(2,1)} %get-tuple-element.26.refs_5_.refs_2_), channel_id=1, source_target_pairs={{1,2},{2,1},{3,4},{4,3},{5,6},{6,5},{9,10},{10,9},{11,12},{12,11},... | collective-permute-start | bytes 1179656 | tf_op jit(solution)/shard_map/ppermute | solution.py:28
  14.5 10.7 %collective-permute-start.3 = (bf16[1,1584,128]{2,1,0:T(8,128)(2,1)}, bf16[1,1584,128]{2,1,0:T(8,128)(2,1)S(1)}, u32[]{:S(2)}, u32[]{:S(2)}) collective-permute-start(bf16[1,1584,128]{2,1,0:T(8,128)(2,1)} %get-tuple-element.25.refs_0_), channel_id=1, source_target_pairs={{32,64},{64,32},{96,128},{128,96},{160,192},{192,160},{33,65},{65,... | collective-permute-start | bytes 1216520 | tf_op jit(solution)/shard_map/ppermute | solution.py:28
  19.1 6.1 %collective-permute-start.2 = (bf16[1,1584,128]{2,1,0:T(8,128)(2,1)}, bf16[1,1584,128]{2,1,0:T(8,128)(2,1)S(1)}, u32[]{:S(2)}, u32[]{:S(2)}) collective-permute-start(bf16[1,1584,128]{2,1,0:T(8,128)(2,1)} %get-tuple-element.25.refs_0_), channel_id=1, source_target_pairs={{0,32},{32,0},{64,96},{96,64},{128,160},{160,128},{192,224},{224,1... | collective-permute-start | bytes 1216520 | tf_op jit(solution)/shard_map/ppermute | solution.py:28
  19.3 14.4 %collective-permute-start.5 = (bf16[2,1584,128]{2,1,0:T(8,128)(2,1)S(1)}, bf16[2,1584,128]{2,1,0:T(8,128)(2,1)S(1)}, u32[]{:S(2)}, u32[]{:S(2)}) collective-permute-start(bf16[2,1584,128]{2,1,0:T(8,128)(2,1)S(1)} %constant_dynamic-update-slice_fusion), channel_id=1, source_target_pairs={{32,64},{64,32},{96,128},{128,96},{160,192},{192,160},{33,65},{65,... | collective-permute-start | bytes 2433032 | tf_op jit(solution)/shard_map/ppermute | solution.py:28
  22.6 11.1 %collective-permute-start.4 = (bf16[2,1584,128]{2,1,0:T(8,128)(2,1)S(1)}, bf16[2,1584,128]{2,1,0:T(8,128)(2,1)S(1)}, u32[]{:S(2)}, u32[]{:S(2)}) collective-permute-start(bf16[2,1584,128]{2,1,0:T(8,128)(2,1)S(1)} %constant_dynamic-update-slice_fusion), channel_id=1, source_target_pairs={{0,32},{32,0},{64,96},{96,64},{128,160},{160,128},{192,224},{224,1... | collective-permute-start | bytes 2433032 | tf_op jit(solution)/shard_map/ppermute | solution.py:28
  46.7 8.0 %collective-permute-start.8 = (bf16[3,256,384]{2,1,0:T(8,128)(2,1)S(1)}, bf16[3,256,384]{2,1,0:T(8,128)(2,1)S(1)}, u32[]{:S(2)}, u32[]{:S(2)}) collective-permute-start(bf16[3,256,384]{2,1,0:T(8,128)(2,1)S(1)} %get-tuple-element.37), channel_id=1, source_target_pairs={{0,32},{32,0},{64,96},{96,64},{128,160},{160,128},{192,224},{224,1... | collective-permute-start | bytes 1769480 | tf_op jit(solution)/shard_map/ppermute | solution.py:28
  47.2 11.5 %collective-permute-start.9 = (bf16[3,256,384]{2,1,0:T(8,128)(2,1)S(1)}, bf16[3,256,384]{2,1,0:T(8,128)(2,1)S(1)}, u32[]{:S(2)}, u32[]{:S(2)}) collective-permute-start(bf16[3,256,384]{2,1,0:T(8,128)(2,1)S(1)} %get-tuple-element.38), channel_id=1, source_target_pairs={{32,64},{64,32},{96,128},{128,96},{160,192},{192,160},{33,65},{65,... | collective-permute-start | bytes 1769480 | tf_op jit(solution)/shard_map/ppermute | solution.py:28
  50.3 20.1 %collective-permute-start.13 = (bf16[2,384,256]{2,1,0:T(8,128)(2,1)S(1)}, bf16[2,384,256]{2,1,0:T(8,128)(2,1)S(1)}, u32[]{:S(2)}, u32[]{:S(2)}) collective-permute-start(bf16[2,384,256]{2,1,0:T(8,128)(2,1)S(1)} %get-tuple-element.43), channel_id=1, source_target_pairs={{1,2},{2,1},{3,4},{4,3},{5,6},{6,5},{9,10},{10,9},{11,12},{12,11},... | collective-permute-start | bytes 1179656 | tf_op jit(solution)/shard_map/ppermute | solution.py:28
  54.6 15.8 %collective-permute-start.12 = (bf16[2,384,256]{2,1,0:T(8,128)(2,1)S(1)}, bf16[2,384,256]{2,1,0:T(8,128)(2,1)S(1)}, u32[]{:S(2)}, u32[]{:S(2)}) collective-permute-start(bf16[2,384,256]{2,1,0:T(8,128)(2,1)S(1)} %get-tuple-element.42), channel_id=1, source_target_pairs={{0,1},{1,0},{2,3},{3,2},{4,5},{5,4},{6,7},{7,6},{8,9},{9,8},{10,11... | collective-permute-start | bytes 1179656 | tf_op jit(solution)/shard_map/ppermute | solution.py:28
  58.9 11.5 %collective-permute-start.11 = (bf16[1,256,384]{2,1,0:T(8,128)(2,1)S(1)}, bf16[1,256,384]{2,1,0:T(8,128)(2,1)S(1)}, u32[]{:S(2)}, u32[]{:S(2)}) collective-permute-start(bf16[1,256,384]{2,1,0:T(8,128)(2,1)S(1)} %get-tuple-element.47), channel_id=1, source_target_pairs={{8,16},{16,8},{9,17},{17,9},{10,18},{18,10},{11,19},{19,11},{12,20... | collective-permute-start | bytes 589832 | tf_op jit(solution)/shard_map/ppermute | solution.py:28
  59.6 19.7 %collective-permute-start.10 = (bf16[1,256,384]{2,1,0:T(8,128)(2,1)S(1)}, bf16[1,256,384]{2,1,0:T(8,128)(2,1)S(1)}, u32[]{:S(2)}, u32[]{:S(2)}) collective-permute-start(bf16[1,256,384]{2,1,0:T(8,128)(2,1)S(1)} %get-tuple-element.48), channel_id=1, source_target_pairs={{0,8},{8,0},{16,24},{24,16},{1,9},{9,1},{17,25},{25,17},{2,10},{10... | collective-permute-start | bytes 589832 | tf_op jit(solution)/shard_map/ppermute | solution.py:28

commit v5 on v4

--- a/solution.py
+++ b/solution.py
@@ -115,7 +115,7 @@
         log = jnp.concatenate([row_of(aux, h) for aux in auxes], axis=1)
         delta = jnp.concatenate([row_of(aux, heads + h) for aux in auxes], axis=1)
         log = log * LOG2_E
-        dq = None
+        turned = []
         for s in range(sides):
             k = kvs[s][0, :, cols]
             v = kvs[s][1, :, cols]
@@ -134,8 +134,9 @@
                 dk = dk + acc_ins[s][0, :, cols]
             accs[s][1, :, cols] = dv.astype(accs[s].dtype)
             accs[s][0, :, cols] = dk.astype(accs[s].dtype)
-            part = dot(k.astype(F32).T.astype(BF16), ds)
-            dq = part if dq is None else dq + part
+            turned.append(k.astype(F32).T.astype(BF16))
+        all_ds = ds_ref[h * sides:(h + 1) * sides].reshape(sides * rows, q.shape[0])
+        dq = dot(jnp.concatenate(turned, axis=1), all_ds)
         for out, group in zip(dqs, groups):
             for at_out, tile in enumerate(group):
                 mine = dq[:, tile * rows:(tile + 1) * rows]

time: 80.6 us -> 80.5 us (level)
  transfers between devices with their start and end apart: 14 -> 14, of which waited for: 4 -> 4; matrix products, arithmetic and copies ran while one was open for 0% -> 0% of each run, Pallas kernels for 17% -> 16%
where the time goes in v5:
time: 80.5 us; the launch traced here: 80.2 us
  starting transfers between devices  39.2 us (49%)
  Pallas kernels  23.4 us (29%)
  waiting for transfers between devices  16.3 us (20%)
  between operations  0.83 us (1%)
    ppermute x14, starting transfers between devices, meet(): return lax.ppermute(x, axis, pairs)  39.2 us
    pallas_call x3, Pallas kernels, run_tiles(): pl.pallas_call(functools.partial(tiles_kernel, sizes, len(kvs), heads, sc...  20.1 us
    ppermute x14, waiting for transfers between devices, meet(): return lax.ppermute(x, axis, pairs)  16.3 us
    pallas_call x1, Pallas kernels, make_payloads(): pl.pallas_call(functools.partial(payload_kernel, heads), in_specs=[pl.Blo...  2.26 us
  transfers between devices with their start and end apart: 14, of which 4 were waited for; matrix products, arithmetic and copies ran while one was open for 0% of the time, Pallas kernels for 16%

profile of v5, /device:TPU:15, one launch (start us, length us, event | category | flops | bytes accessed | tf_op | source)
XLA Modules:
  0.0 80.2 jit_solution(10416988278286854960)
XLA Ops:
  0.6 2.3 %payloads.1 = (bf16[1,1584,128]{2,1,0:T(8,128)(2,1)}, bf16[2,384,256]{2,1,0:T(8,128)(2,1)}) custom-call(bf16[384,256]{1,0:T(8,128)(2,1)} %bitcast.9, bf16[384,256]{1,0:T(8,128)(2,1)} %bitcast.10, bf16[384,256]{1,0:T(8,128)(2,1)} %bitcast.11, f32[2,384]{1,0:T(2,128)} %bitcast.14, bf16[384,256]{1,0:T(8,128)(2,1)} %bitcast.12, bf16[384,256]{1,0:T(8,128)(2,1)} %bitcast.13), custom_call_target="tpu_custom_call" | custom-call | tf_op jit(solution)/shard_map/payloads/pallas_call | solution.py:73
  2.9 1.7 %collective-permute-start = (bf16[1,1584,128]{2,1,0:T(8,128)(2,1)}, bf16[1,1584,128]{2,1,0:T(8,128)(2,1)S(1)}, u32[]{:S(2)}, u32[]{:S(2)}) collective-permute-start(bf16[1,1584,128]{2,1,0:T(8,128)(2,1)} %get-tuple-element.25.refs_0_), channel_id=1, source_target_pairs={{0,8},{8,0},{16,24},{24,16},{1,9},{9,1},{17,25},{25,17},{2,10},{10... | collective-permute-start | bytes 1216520 | tf_op jit(solution)/shard_map/ppermute | solution.py:28
  4.6 0.7 collective-permute-start.1
  5.3 0.6 collective-permute-start.7
  6.0 8.5 %collective-permute-start.6 = (bf16[2,384,256]{2,1,0:T(8,128)(2,1)}, bf16[2,384,256]{2,1,0:T(8,128)(2,1)S(1)}, u32[]{:S(2)}, u32[]{:S(2)}) collective-permute-start(bf16[2,384,256]{2,1,0:T(8,128)(2,1)} %get-tuple-element.26.refs_5_.refs_2_), channel_id=1, source_target_pairs={{1,2},{2,1},{3,4},{4,3},{5,6},{6,5},{9,10},{10,9},{11,12},{12,11},... | collective-permute-start | bytes 1179656 | tf_op jit(solution)/shard_map/ppermute | solution.py:28
  14.5 4.6 %collective-permute-start.3 = (bf16[1,1584,128]{2,1,0:T(8,128)(2,1)}, bf16[1,1584,128]{2,1,0:T(8,128)(2,1)S(1)}, u32[]{:S(2)}, u32[]{:S(2)}) collective-permute-start(bf16[1,1584,128]{2,1,0:T(8,128)(2,1)} %get-tuple-element.25.refs_0_), channel_id=1, source_target_pairs={{32,64},{64,32},{96,128},{128,96},{160,192},{192,160},{33,65},{65,... | collective-permute-start | bytes 1216520 | tf_op jit(solution)/shard_map/ppermute | solution.py:28
  19.3 3.3 %collective-permute-start.5 = (bf16[2,1584,128]{2,1,0:T(8,128)(2,1)S(1)}, bf16[2,1584,128]{2,1,0:T(8,128)(2,1)S(1)}, u32[]{:S(2)}, u32[]{:S(2)}) collective-permute-start(bf16[2,1584,128]{2,1,0:T(8,128)(2,1)S(1)} %constant_dynamic-update-slice_fusion), channel_id=1, source_target_pairs={{32,64},{64,32},{96,128},{128,96},{160,192},{192,160},{33,65},{65,... | collective-permute-start | bytes 2433032 | tf_op jit(solution)/shard_map/ppermute | solution.py:28
  22.6 0.3 collective-permute-start.4
  22.9 2.3 %collective-permute-done.3.refs_4_ = bf16[1,1584,128]{2,1,0:T(8,128)(2,1)S(1)} collective-permute-done((bf16[1,1584,128]{2,1,0:T(8,128)(2,1)}, bf16[1,1584,128]{2,1,0:T(8,128)(2,1)S(1)}, u32[]{:S(2)}, u32[]{:S(2)}) %collective-permute-start.3) | collective-permute-done | bytes 405536 | tf_op jit(solution)/shard_map/ppermute | solution.py:28
  25.2 7.3 %tiles.3 = (f32[1,256,384]{2,1,0:T(8,128)S(1)}, f32[1,256,384]{2,1,0:T(8,128)S(1)}, f32[1,256,384]{2,1,0:T(8,128)S(1)}, f32[1,256,384]{2,1,0:T(8,128)S(1)}, f32[...) custom-call(bf16[1,1584,128]{2,1,0:T(8,128)(2,1)S(1)} %copy-done, ...), custom_call_target="tpu_custom_call" | custom-call | flops 11324620800 | tf_op jit(solution)/shard_map/tiles/pallas_call | solution.py:153
  32.5 1.2 %collective-permute-done.5.refs_1_.refs_6_ = bf16[2,1584,128]{2,1,0:T(8,128)(2,1)S(1)} collective-permute-done((bf16[2,1584,128]{2,1,0:T(8,128)(2,1)S(1)}, bf16[2,1584,128]{2,1,0:T(8,128)(2,1)S(1)}, u32[]{:S(2)}, u32[]{:S(2)}) %collective-permute-start.5) | collective-permute-done | bytes 811040 | tf_op jit(solution)/shard_map/ppermute | solution.py:28
  33.7 5.8 %tiles.4 = (f32[2,256,384]{2,1,0:T(8,128)S(1)}, f32[2,256,384]{2,1,0:T(8,128)S(1)}, f32[2,384,256]{2,1,0:T(8,128)S(1)}, bf16[2,384,256]{2,1,0:T(8,128)(2,1)S(1)}) custom-call(bf16[2,1584,128]{2,1,0:T(8,128)(2,1)S(1)} %collective-permute-done.4.refs_0_.refs_5_, bf16[2,1584,128]{2,1,0:T(8,128)(2,1)S(1)} %collective-permute-done.5.refs_1_.refs_6_, ...), custom_call_target="tpu_custom_call" | custom-call | tf_op jit(solution)/shard_map/tiles/pallas_call | solution.py:153
  39.5 7.1 %tiles.5 = (f32[1,256,384]{2,1,0:T(8,128)S(1)}, f32[1,256,384]{2,1,0:T(8,128)S(1)}, f32[1,256,384]{2,1,0:T(8,128)S(1)}, bf16[3,256,384]{2,1,0:T(8,128)(2,1)S(1)}...) custom-call(bf16[1,1584,128]{2,1,0:T(8,128)(2,1)S(1)} %copy-done, ...), custom_call_target="tpu_custom_call" | custom-call | tf_op jit(solution)/shard_map/tiles/pallas_call | solution.py:153
  46.6 0.5 collective-permute-start.8
  47.0 3.1 %collective-permute-start.9 = (bf16[3,256,384]{2,1,0:T(8,128)(2,1)S(1)}, bf16[3,256,384]{2,1,0:T(8,128)(2,1)S(1)}, u32[]{:S(2)}, u32[]{:S(2)}) collective-permute-start(bf16[3,256,384]{2,1,0:T(8,128)(2,1)S(1)} %get-tuple-element.38), channel_id=1, source_target_pairs={{32,64},{64,32},{96,128},{128,96},{160,192},{192,160},{33,65},{65,... | collective-permute-start | bytes 1769480 | tf_op jit(solution)/shard_map/ppermute | solution.py:28
  50.1 4.3 %collective-permute-start.13 = (bf16[2,384,256]{2,1,0:T(8,128)(2,1)S(1)}, bf16[2,384,256]{2,1,0:T(8,128)(2,1)S(1)}, u32[]{:S(2)}, u32[]{:S(2)}) collective-permute-start(bf16[2,384,256]{2,1,0:T(8,128)(2,1)S(1)} %get-tuple-element.43), channel_id=1, source_target_pairs={{1,2},{2,1},{3,4},{4,3},{5,6},{6,5},{9,10},{10,9},{11,12},{12,11},... | collective-permute-start | bytes 1179656 | tf_op jit(solution)/shard_map/ppermute | solution.py:28
  54.5 0.1 collective-permute-start.12
  54.6 4.0 %collective-permute-done.9.b_ref = bf16[3,256,384]{2,1,0:T(8,128)(2,1)S(1)} collective-permute-done((bf16[3,256,384]{2,1,0:T(8,128)(2,1)S(1)}, bf16[3,256,384]{2,1,0:T(8,128)(2,1)S(1)}, u32[]{:S(2)}, u32[]{:S(2)}) %collective-permute-start.9) | collective-permute-done | bytes 589856 | tf_op jit(solution)/shard_map/ppermute | solution.py:28
  58.5 0.1 convert_add_fusion
  58.7 0.1 fusion
  58.8 0.7 collective-permute-start.11
  59.4 10.8 %collective-permute-start.10 = (bf16[1,256,384]{2,1,0:T(8,128)(2,1)S(1)}, bf16[1,256,384]{2,1,0:T(8,128)(2,1)S(1)}, u32[]{:S(2)}, u32[]{:S(2)}) collective-permute-start(bf16[1,256,384]{2,1,0:T(8,128)(2,1)S(1)} %get-tuple-element.48), channel_id=1, source_target_pairs={{0,8},{8,0},{16,24},{24,16},{1,9},{9,1},{17,25},{25,17},{2,10},{10... | collective-permute-start | bytes 589832 | tf_op jit(solution)/shard_map/ppermute | solution.py:28
  70.3 8.8 %collective-permute-done.10.row_a_ref = bf16[1,256,384]{2,1,0:T(8,128)(2,1)S(1)} collective-permute-done((bf16[1,256,384]{2,1,0:T(8,128)(2,1)S(1)}, bf16[1,256,384]{2,1,0:T(8,128)(2,1)S(1)}, u32[]{:S(2)}, u32[]{:S(2)}) %collective-permute-start.10) | collective-permute-done | bytes 196640 | tf_op jit(solution)/shard_map/ppermute | solution.py:28
  79.1 1.1 %finish.1 = (bf16[384,256]{1,0:T(8,128)(2,1)}, bf16[384,256]{1,0:T(8,128)(2,1)}, bf16[384,256]{1,0:T(8,128)(2,1)}) custom-call(f32[1,256,384]{2,1,0:T(8,128)S(1)} %get-tuple-element.36.dq_ref, bf16[3,256,384]{2,1,0:T(8,128)(2,1)S(1)} %collective-permute-done.8.a_ref, bf16[3,256,384]{2,1,0:T(8,128)(2,1)S(1)} %collective-permute-done.9.b_ref, ...), custom_call_target="tpu_custom_call" | custom-call | tf_op jit(solution)/shard_map/finish/pallas_call | solution.py:183
  (17 shorter events, 0.2 us)
Async XLA Ops:
  2.9 22.3 %copy-start = (bf16[1,1584,128]{2,1,0:T(8,128)(2,1)S(1)}, bf16[1,1584,128]{2,1,0:T(8,128)(2,1)}, u32[]{:S(2)}) copy-start(bf16[1,1584,128]{2,1,0:T(8,128)(2,1)} %get-tuple-element.25.refs_0_) | copy-start | bytes 1216516
  2.9 22.2 %copy-start.1 = (bf16[2,384,256]{2,1,0:T(8,128)(2,1)S(1)}, bf16[2,384,256]{2,1,0:T(8,128)(2,1)}, u32[]{:S(2)}) copy-start(bf16[2,384,256]{2,1,0:T(8,128)(2,1)} %get-tuple-element.26.refs_5_.refs_2_) | copy-start | bytes 1179652
  2.9 16.1 %collective-permute-start = (bf16[1,1584,128]{2,1,0:T(8,128)(2,1)}, bf16[1,1584,128]{2,1,0:T(8,128)(2,1)S(1)}, u32[]{:S(2)}, u32[]{:S(2)}) collective-permute-start(bf16[1,1584,128]{2,1,0:T(8,128)(2,1)} %get-tuple-element.25.refs_0_), channel_id=1, source_target_pairs={{0,8},{8,0},{16,24},{24,16},{1,9},{9,1},{17,25},{25,17},{2,10},{10... | collective-permute-start | bytes 1216520 | tf_op jit(solution)/shard_map/ppermute | solution.py:28
  4.6 14.6 %collective-permute-start.1 = (bf16[1,1584,128]{2,1,0:T(8,128)(2,1)}, bf16[1,1584,128]{2,1,0:T(8,128)(2,1)S(1)}, u32[]{:S(2)}, u32[]{:S(2)}) collective-permute-start(bf16[1,1584,128]{2,1,0:T(8,128)(2,1)} %get-tuple-element.25.refs_0_), channel_id=1, source_target_pairs={{8,16},{16,8},{9,17},{17,9},{10,18},{18,10},{11,19},{19,11},{12,20... | collective-permute-start | bytes 1216520 | tf_op jit(solution)/shard_map/ppermute | solution.py:28
  5.3 17.3 %collective-permute-start.7 = (bf16[2,384,256]{2,1,0:T(8,128)(2,1)}, bf16[2,384,256]{2,1,0:T(8,128)(2,1)S(1)}, u32[]{:S(2)}, u32[]{:S(2)}) collective-permute-start(bf16[2,384,256]{2,1,0:T(8,128)(2,1)} %get-tuple-element.26.refs_5_.refs_2_), channel_id=1, source_target_pairs={{0,1},{1,0},{2,3},{3,2},{4,5},{5,4},{6,7},{7,6},{8,9},{9,8},{10,11... | collective-permute-start | bytes 1179656 | tf_op jit(solution)/shard_map/ppermute | solution.py:28
  6.0 33.5 %collective-permute-start.6 = (bf16[2,384,256]{2,1,0:T(8,128)(2,1)}, bf16[2,384,256]{2,1,0:T(8,128)(2,1)S(1)}, u32[]{:S(2)}, u32[]{:S(2)}) collective-permute-start(bf16[2,384,256]{2,1,0:T(8,128)(2,1)} %get-tuple-element.26.refs_5_.refs_2_), channel_id=1, source_target_pairs={{1,2},{2,1},{3,4},{4,3},{5,6},{6,5},{9,10},{10,9},{11,12},{12,11},... | collective-permute-start | bytes 1179656 | tf_op jit(solution)/shard_map/ppermute | solution.py:28
  14.5 10.7 %collective-permute-start.3 = (bf16[1,1584,128]{2,1,0:T(8,128)(2,1)}, bf16[1,1584,128]{2,1,0:T(8,128)(2,1)S(1)}, u32[]{:S(2)}, u32[]{:S(2)}) collective-permute-start(bf16[1,1584,128]{2,1,0:T(8,128)(2,1)} %get-tuple-element.25.refs_0_), channel_id=1, source_target_pairs={{32,64},{64,32},{96,128},{128,96},{160,192},{192,160},{33,65},{65,... | collective-permute-start | bytes 1216520 | tf_op jit(solution)/shard_map/ppermute | solution.py:28
  19.1 6.1 %collective-permute-start.2 = (bf16[1,1584,128]{2,1,0:T(8,128)(2,1)}, bf16[1,1584,128]{2,1,0:T(8,128)(2,1)S(1)}, u32[]{:S(2)}, u32[]{:S(2)}) collective-permute-start(bf16[1,1584,128]{2,1,0:T(8,128)(2,1)} %get-tuple-element.25.refs_0_), channel_id=1, source_target_pairs={{0,32},{32,0},{64,96},{96,64},{128,160},{160,128},{192,224},{224,1... | collective-permute-start | bytes 1216520 | tf_op jit(solution)/shard_map/ppermute | solution.py:28
  19.3 14.4 %collective-permute-start.5 = (bf16[2,1584,128]{2,1,0:T(8,128)(2,1)S(1)}, bf16[2,1584,128]{2,1,0:T(8,128)(2,1)S(1)}, u32[]{:S(2)}, u32[]{:S(2)}) collective-permute-start(bf16[2,1584,128]{2,1,0:T(8,128)(2,1)S(1)} %constant_dynamic-update-slice_fusion), channel_id=1, source_target_pairs={{32,64},{64,32},{96,128},{128,96},{160,192},{192,160},{33,65},{65,... | collective-permute-start | bytes 2433032 | tf_op jit(solution)/shard_map/ppermute | solution.py:28
  22.6 11.1 %collective-permute-start.4 = (bf16[2,1584,128]{2,1,0:T(8,128)(2,1)S(1)}, bf16[2,1584,128]{2,1,0:T(8,128)(2,1)S(1)}, u32[]{:S(2)}, u32[]{:S(2)}) collective-permute-start(bf16[2,1584,128]{2,1,0:T(8,128)(2,1)S(1)} %constant_dynamic-update-slice_fusion), channel_id=1, source_target_pairs={{0,32},{32,0},{64,96},{96,64},{128,160},{160,128},{192,224},{224,1... | collective-permute-start | bytes 2433032 | tf_op jit(solution)/shard_map/ppermute | solution.py:28
  46.6 8.0 %collective-permute-start.8 = (bf16[3,256,384]{2,1,0:T(8,128)(2,1)S(1)}, bf16[3,256,384]{2,1,0:T(8,128)(2,1)S(1)}, u32[]{:S(2)}, u32[]{:S(2)}) collective-permute-start(bf16[3,256,384]{2,1,0:T(8,128)(2,1)S(1)} %get-tuple-element.37), channel_id=1, source_target_pairs={{0,32},{32,0},{64,96},{96,64},{128,160},{160,128},{192,224},{224,1... | collective-permute-start | bytes 1769480 | tf_op jit(solution)/shard_map/ppermute | solution.py:28
  47.0 11.5 %collective-permute-start.9 = (bf16[3,256,384]{2,1,0:T(8,128)(2,1)S(1)}, bf16[3,256,384]{2,1,0:T(8,128)(2,1)S(1)}, u32[]{:S(2)}, u32[]{:S(2)}) collective-permute-start(bf16[3,256,384]{2,1,0:T(8,128)(2,1)S(1)} %get-tuple-element.38), channel_id=1, source_target_pairs={{32,64},{64,32},{96,128},{128,96},{160,192},{192,160},{33,65},{65,... | collective-permute-start | bytes 1769480 | tf_op jit(solution)/shard_map/ppermute | solution.py:28
  50.1 20.1 %collective-permute-start.13 = (bf16[2,384,256]{2,1,0:T(8,128)(2,1)S(1)}, bf16[2,384,256]{2,1,0:T(8,128)(2,1)S(1)}, u32[]{:S(2)}, u32[]{:S(2)}) collective-permute-start(bf16[2,384,256]{2,1,0:T(8,128)(2,1)S(1)} %get-tuple-element.43), channel_id=1, source_target_pairs={{1,2},{2,1},{3,4},{4,3},{5,6},{6,5},{9,10},{10,9},{11,12},{12,11},... | collective-permute-start | bytes 1179656 | tf_op jit(solution)/shard_map/ppermute | solution.py:28
  54.5 15.8 %collective-permute-start.12 = (bf16[2,384,256]{2,1,0:T(8,128)(2,1)S(1)}, bf16[2,384,256]{2,1,0:T(8,128)(2,1)S(1)}, u32[]{:S(2)}, u32[]{:S(2)}) collective-permute-start(bf16[2,384,256]{2,1,0:T(8,128)(2,1)S(1)} %get-tuple-element.42), channel_id=1, source_target_pairs={{0,1},{1,0},{2,3},{3,2},{4,5},{5,4},{6,7},{7,6},{8,9},{9,8},{10,11... | collective-permute-start | bytes 1179656 | tf_op jit(solution)/shard_map/ppermute | solution.py:28
  58.8 11.5 %collective-permute-start.11 = (bf16[1,256,384]{2,1,0:T(8,128)(2,1)S(1)}, bf16[1,256,384]{2,1,0:T(8,128)(2,1)S(1)}, u32[]{:S(2)}, u32[]{:S(2)}) collective-permute-start(bf16[1,256,384]{2,1,0:T(8,128)(2,1)S(1)} %get-tuple-element.47), channel_id=1, source_target_pairs={{8,16},{16,8},{9,17},{17,9},{10,18},{18,10},{11,19},{19,11},{12,20... | collective-permute-start | bytes 589832 | tf_op jit(solution)/shard_map/ppermute | solution.py:28
  59.4 19.7 %collective-permute-start.10 = (bf16[1,256,384]{2,1,0:T(8,128)(2,1)S(1)}, bf16[1,256,384]{2,1,0:T(8,128)(2,1)S(1)}, u32[]{:S(2)}, u32[]{:S(2)}) collective-permute-start(bf16[1,256,384]{2,1,0:T(8,128)(2,1)S(1)} %get-tuple-element.48), channel_id=1, source_target_pairs={{0,8},{8,0},{16,24},{24,16},{1,9},{9,1},{17,25},{25,17},{2,10},{10... | collective-permute-start | bytes 589832 | tf_op jit(solution)/shard_map/ppermute | solution.py:28

commit v6 on v5

--- a/solution.py
+++ b/solution.py
@@ -221,11 +221,11 @@
     far_dqs, (dkv, to_a) = work(
         far, [own_kv, kv_a], acc_in=accs, groups=[[0, 1], [2, 3]], kinds=[F32] * 2, acc_kinds=[F32, BF16], weight=0
     )
-    (dq_own, dq_row_a, dq_row_b, dq_frame_a, dq_frame_b), (to_b,) = work(
+    (dq_own, dq_row_a, dq_row_b, dq_frame_b, dq_frame_a), (to_b,) = work(
         near + far,
         [kv_b],
         dq_in=[*near_dqs, *far_dqs],
-        groups=[[0], [1], [2], [3, 5, 6], [4, 7, 8]],
+        groups=[[0], [1], [2], [4, 7, 8], [3, 5, 6]],
         kinds=[F32] * 3 + [BF16] * 2,
         acc_kinds=[BF16],
         weight=0,
@@ -235,10 +235,10 @@
     dkv_a = meet(to_a, "col", 0)
     back_b = meet(dq_frame_b, "frame", 1)
     back_a = meet(dq_frame_a, "frame", 0)
-    back = back_b.astype(F32) + back_a.astype(F32)
+    back = back_a.astype(F32) + back_b.astype(F32)
     row_back_b = meet((dq_row_b + back[2:3]).astype(BF16), "row", 1)
     row_back_a = meet((dq_row_a + back[1:2]).astype(BF16), "row", 0)
-    grads = finish(dq_own, back_a, back_b, row_back_a, row_back_b, dkv, dkv_a, dkv_b, scale)
+    grads = finish(dq_own, back_b, back_a, row_back_a, row_back_b, dkv, dkv_a, dkv_b, scale)
     return tuple(grad.reshape(queries.shape) for grad in grads)
 
 

time: 80.5 us -> 80.4 us (level)
  no operation moved by 1% of the time
where the time goes in v6:
time: 80.4 us; the launch traced here: 79.7 us
  starting transfers between devices  38.7 us (48%)
  Pallas kernels  23.4 us (29%)
  waiting for transfers between devices  16.4 us (20%)
  between operations  0.83 us (1%)
    ppermute x14, starting transfers between devices, meet(): return lax.ppermute(x, axis, pairs)  38.7 us
    pallas_call x3, Pallas kernels, run_tiles(): pl.pallas_call(functools.partial(tiles_kernel, sizes, len(kvs), heads, sc...  20.1 us
    ppermute x14, waiting for transfers between devices, meet(): return lax.ppermute(x, axis, pairs)  16.4 us
    pallas_call x1, Pallas kernels, make_payloads(): pl.pallas_call(functools.partial(payload_kernel, heads), in_specs=[pl.Blo...  2.26 us
  transfers between devices with their start and end apart: 14, of which 4 were waited for; matrix products, arithmetic and copies ran while one was open for 0% of the time, Pallas kernels for 16%

profile of v6, /device:TPU:15, one launch (start us, length us, event | category | flops | bytes accessed | tf_op | source)
XLA Modules:
  0.0 79.7 jit_solution(16399278392650188123)
XLA Ops:
  0.6 2.3 %payloads.1 = (bf16[1,1584,128]{2,1,0:T(8,128)(2,1)}, bf16[2,384,256]{2,1,0:T(8,128)(2,1)}) custom-call(bf16[384,256]{1,0:T(8,128)(2,1)} %bitcast.9, bf16[384,256]{1,0:T(8,128)(2,1)} %bitcast.10, bf16[384,256]{1,0:T(8,128)(2,1)} %bitcast.11, f32[2,384]{1,0:T(2,128)} %bitcast.14, bf16[384,256]{1,0:T(8,128)(2,1)} %bitcast.12, bf16[384,256]{1,0:T(8,128)(2,1)} %bitcast.13), custom_call_target="tpu_custom_call" | custom-call | tf_op jit(solution)/shard_map/payloads/pallas_call | solution.py:73
  2.9 1.7 %collective-permute-start = (bf16[1,1584,128]{2,1,0:T(8,128)(2,1)}, bf16[1,1584,128]{2,1,0:T(8,128)(2,1)S(1)}, u32[]{:S(2)}, u32[]{:S(2)}) collective-permute-start(bf16[1,1584,128]{2,1,0:T(8,128)(2,1)} %get-tuple-element.25.refs_0_), channel_id=1, source_target_pairs={{0,8},{8,0},{16,24},{24,16},{1,9},{9,1},{17,25},{25,17},{2,10},{10... | collective-permute-start | bytes 1216520 | tf_op jit(solution)/shard_map/ppermute | solution.py:28
  4.6 0.7 collective-permute-start.1
  5.3 0.6 collective-permute-start.7
  6.0 8.5 %collective-permute-start.6 = (bf16[2,384,256]{2,1,0:T(8,128)(2,1)}, bf16[2,384,256]{2,1,0:T(8,128)(2,1)S(1)}, u32[]{:S(2)}, u32[]{:S(2)}) collective-permute-start(bf16[2,384,256]{2,1,0:T(8,128)(2,1)} %get-tuple-element.26.refs_5_.refs_2_), channel_id=1, source_target_pairs={{1,2},{2,1},{3,4},{4,3},{5,6},{6,5},{9,10},{10,9},{11,12},{12,11},... | collective-permute-start | bytes 1179656 | tf_op jit(solution)/shard_map/ppermute | solution.py:28
  14.5 4.6 %collective-permute-start.3 = (bf16[1,1584,128]{2,1,0:T(8,128)(2,1)}, bf16[1,1584,128]{2,1,0:T(8,128)(2,1)S(1)}, u32[]{:S(2)}, u32[]{:S(2)}) collective-permute-start(bf16[1,1584,128]{2,1,0:T(8,128)(2,1)} %get-tuple-element.25.refs_0_), channel_id=1, source_target_pairs={{32,64},{64,32},{96,128},{128,96},{160,192},{192,160},{33,65},{65,... | collective-permute-start | bytes 1216520 | tf_op jit(solution)/shard_map/ppermute | solution.py:28
  19.3 3.3 %collective-permute-start.5 = (bf16[2,1584,128]{2,1,0:T(8,128)(2,1)S(1)}, bf16[2,1584,128]{2,1,0:T(8,128)(2,1)S(1)}, u32[]{:S(2)}, u32[]{:S(2)}) collective-permute-start(bf16[2,1584,128]{2,1,0:T(8,128)(2,1)S(1)} %constant_dynamic-update-slice_fusion), channel_id=1, source_target_pairs={{32,64},{64,32},{96,128},{128,96},{160,192},{192,160},{33,65},{65,... | collective-permute-start | bytes 2433032 | tf_op jit(solution)/shard_map/ppermute | solution.py:28
  22.6 0.3 collective-permute-start.4
  22.9 2.3 %collective-permute-done.3.refs_4_ = bf16[1,1584,128]{2,1,0:T(8,128)(2,1)S(1)} collective-permute-done((bf16[1,1584,128]{2,1,0:T(8,128)(2,1)}, bf16[1,1584,128]{2,1,0:T(8,128)(2,1)S(1)}, u32[]{:S(2)}, u32[]{:S(2)}) %collective-permute-start.3) | collective-permute-done | bytes 405536 | tf_op jit(solution)/shard_map/ppermute | solution.py:28
  25.2 7.3 %tiles.3 = (f32[1,256,384]{2,1,0:T(8,128)S(1)}, f32[1,256,384]{2,1,0:T(8,128)S(1)}, f32[1,256,384]{2,1,0:T(8,128)S(1)}, f32[1,256,384]{2,1,0:T(8,128)S(1)}, f32[...) custom-call(bf16[1,1584,128]{2,1,0:T(8,128)(2,1)S(1)} %copy-done, ...), custom_call_target="tpu_custom_call" | custom-call | flops 11324620800 | tf_op jit(solution)/shard_map/tiles/pallas_call | solution.py:153
  32.5 1.2 %collective-permute-done.5.refs_1_.refs_6_ = bf16[2,1584,128]{2,1,0:T(8,128)(2,1)S(1)} collective-permute-done((bf16[2,1584,128]{2,1,0:T(8,128)(2,1)S(1)}, bf16[2,1584,128]{2,1,0:T(8,128)(2,1)S(1)}, u32[]{:S(2)}, u32[]{:S(2)}) %collective-permute-start.5) | collective-permute-done | bytes 811040 | tf_op jit(solution)/shard_map/ppermute | solution.py:28
  33.7 5.8 %tiles.4 = (f32[2,256,384]{2,1,0:T(8,128)S(1)}, f32[2,256,384]{2,1,0:T(8,128)S(1)}, f32[2,384,256]{2,1,0:T(8,128)S(1)}, bf16[2,384,256]{2,1,0:T(8,128)(2,1)S(1)}) custom-call(bf16[2,1584,128]{2,1,0:T(8,128)(2,1)S(1)} %collective-permute-done.4.refs_0_.refs_5_, bf16[2,1584,128]{2,1,0:T(8,128)(2,1)S(1)} %collective-permute-done.5.refs_1_.refs_6_, ...), custom_call_target="tpu_custom_call" | custom-call | tf_op jit(solution)/shard_map/tiles/pallas_call | solution.py:153
  39.5 7.1 %tiles.5 = (f32[1,256,384]{2,1,0:T(8,128)S(1)}, f32[1,256,384]{2,1,0:T(8,128)S(1)}, f32[1,256,384]{2,1,0:T(8,128)S(1)}, bf16[3,256,384]{2,1,0:T(8,128)(2,1)S(1)}...) custom-call(bf16[1,1584,128]{2,1,0:T(8,128)(2,1)S(1)} %copy-done, ...), custom_call_target="tpu_custom_call" | custom-call | tf_op jit(solution)/shard_map/tiles/pallas_call | solution.py:153
  46.6 3.5 %collective-permute-start.8 = (bf16[3,256,384]{2,1,0:T(8,128)(2,1)S(1)}, bf16[3,256,384]{2,1,0:T(8,128)(2,1)S(1)}, u32[]{:S(2)}, u32[]{:S(2)}) collective-permute-start(bf16[3,256,384]{2,1,0:T(8,128)(2,1)S(1)} %get-tuple-element.37), channel_id=1, source_target_pairs={{32,64},{64,32},{96,128},{128,96},{160,192},{192,160},{33,65},{65,... | collective-permute-start | bytes 1769480 | tf_op jit(solution)/shard_map/ppermute | solution.py:28
  50.0 0.1 collective-permute-start.9
  50.1 3.8 %collective-permute-start.13 = (bf16[2,384,256]{2,1,0:T(8,128)(2,1)S(1)}, bf16[2,384,256]{2,1,0:T(8,128)(2,1)S(1)}, u32[]{:S(2)}, u32[]{:S(2)}) collective-permute-start(bf16[2,384,256]{2,1,0:T(8,128)(2,1)S(1)} %get-tuple-element.43), channel_id=1, source_target_pairs={{1,2},{2,1},{3,4},{4,3},{5,6},{6,5},{9,10},{10,9},{11,12},{12,11},... | collective-permute-start | bytes 1179656 | tf_op jit(solution)/shard_map/ppermute | solution.py:28
  54.0 0.1 collective-permute-start.12
  54.1 4.0 %collective-permute-done.8.a_ref = bf16[3,256,384]{2,1,0:T(8,128)(2,1)S(1)} collective-permute-done((bf16[3,256,384]{2,1,0:T(8,128)(2,1)S(1)}, bf16[3,256,384]{2,1,0:T(8,128)(2,1)S(1)}, u32[]{:S(2)}, u32[]{:S(2)}) %collective-permute-start.8) | collective-permute-done | bytes 589856 | tf_op jit(solution)/shard_map/ppermute | solution.py:28
  58.1 0.1 convert_add_fusion
  58.2 0.1 fusion
  58.3 0.7 collective-permute-start.11
  59.0 10.8 %collective-permute-start.10 = (bf16[1,256,384]{2,1,0:T(8,128)(2,1)S(1)}, bf16[1,256,384]{2,1,0:T(8,128)(2,1)S(1)}, u32[]{:S(2)}, u32[]{:S(2)}) collective-permute-start(bf16[1,256,384]{2,1,0:T(8,128)(2,1)S(1)} %get-tuple-element.48), channel_id=1, source_target_pairs={{0,8},{8,0},{16,24},{24,16},{1,9},{9,1},{17,25},{25,17},{2,10},{10... | collective-permute-start | bytes 589832 | tf_op jit(solution)/shard_map/ppermute | solution.py:28
  69.8 8.9 %collective-permute-done.10.row_a_ref = bf16[1,256,384]{2,1,0:T(8,128)(2,1)S(1)} collective-permute-done((bf16[1,256,384]{2,1,0:T(8,128)(2,1)S(1)}, bf16[1,256,384]{2,1,0:T(8,128)(2,1)S(1)}, u32[]{:S(2)}, u32[]{:S(2)}) %collective-permute-start.10) | collective-permute-done | bytes 196640 | tf_op jit(solution)/shard_map/ppermute | solution.py:28
  78.7 1.1 %finish.1 = (bf16[384,256]{1,0:T(8,128)(2,1)}, bf16[384,256]{1,0:T(8,128)(2,1)}, bf16[384,256]{1,0:T(8,128)(2,1)}) custom-call(f32[1,256,384]{2,1,0:T(8,128)S(1)} %get-tuple-element.36.dq_ref, bf16[3,256,384]{2,1,0:T(8,128)(2,1)S(1)} %collective-permute-done.8.a_ref, bf16[3,256,384]{2,1,0:T(8,128)(2,1)S(1)} %collective-permute-done.9.b_ref, ...), custom_call_target="tpu_custom_call" | custom-call | tf_op jit(solution)/shard_map/finish/pallas_call | solution.py:183
  (17 shorter events, 0.2 us)
Async XLA Ops:
  2.9 22.3 %copy-start = (bf16[1,1584,128]{2,1,0:T(8,128)(2,1)S(1)}, bf16[1,1584,128]{2,1,0:T(8,128)(2,1)}, u32[]{:S(2)}) copy-start(bf16[1,1584,128]{2,1,0:T(8,128)(2,1)} %get-tuple-element.25.refs_0_) | copy-start | bytes 1216516
  2.9 22.2 %copy-start.1 = (bf16[2,384,256]{2,1,0:T(8,128)(2,1)S(1)}, bf16[2,384,256]{2,1,0:T(8,128)(2,1)}, u32[]{:S(2)}) copy-start(bf16[2,384,256]{2,1,0:T(8,128)(2,1)} %get-tuple-element.26.refs_5_.refs_2_) | copy-start | bytes 1179652
  2.9 16.1 %collective-permute-start = (bf16[1,1584,128]{2,1,0:T(8,128)(2,1)}, bf16[1,1584,128]{2,1,0:T(8,128)(2,1)S(1)}, u32[]{:S(2)}, u32[]{:S(2)}) collective-permute-start(bf16[1,1584,128]{2,1,0:T(8,128)(2,1)} %get-tuple-element.25.refs_0_), channel_id=1, source_target_pairs={{0,8},{8,0},{16,24},{24,16},{1,9},{9,1},{17,25},{25,17},{2,10},{10... | collective-permute-start | bytes 1216520 | tf_op jit(solution)/shard_map/ppermute | solution.py:28
  4.6 14.6 %collective-permute-start.1 = (bf16[1,1584,128]{2,1,0:T(8,128)(2,1)}, bf16[1,1584,128]{2,1,0:T(8,128)(2,1)S(1)}, u32[]{:S(2)}, u32[]{:S(2)}) collective-permute-start(bf16[1,1584,128]{2,1,0:T(8,128)(2,1)} %get-tuple-element.25.refs_0_), channel_id=1, source_target_pairs={{8,16},{16,8},{9,17},{17,9},{10,18},{18,10},{11,19},{19,11},{12,20... | collective-permute-start | bytes 1216520 | tf_op jit(solution)/shard_map/ppermute | solution.py:28
  5.3 17.3 %collective-permute-start.7 = (bf16[2,384,256]{2,1,0:T(8,128)(2,1)}, bf16[2,384,256]{2,1,0:T(8,128)(2,1)S(1)}, u32[]{:S(2)}, u32[]{:S(2)}) collective-permute-start(bf16[2,384,256]{2,1,0:T(8,128)(2,1)} %get-tuple-element.26.refs_5_.refs_2_), channel_id=1, source_target_pairs={{0,1},{1,0},{2,3},{3,2},{4,5},{5,4},{6,7},{7,6},{8,9},{9,8},{10,11... | collective-permute-start | bytes 1179656 | tf_op jit(solution)/shard_map/ppermute | solution.py:28
  6.0 33.5 %collective-permute-start.6 = (bf16[2,384,256]{2,1,0:T(8,128)(2,1)}, bf16[2,384,256]{2,1,0:T(8,128)(2,1)S(1)}, u32[]{:S(2)}, u32[]{:S(2)}) collective-permute-start(bf16[2,384,256]{2,1,0:T(8,128)(2,1)} %get-tuple-element.26.refs_5_.refs_2_), channel_id=1, source_target_pairs={{1,2},{2,1},{3,4},{4,3},{5,6},{6,5},{9,10},{10,9},{11,12},{12,11},... | collective-permute-start | bytes 1179656 | tf_op jit(solution)/shard_map/ppermute | solution.py:28
  14.5 10.7 %collective-permute-start.3 = (bf16[1,1584,128]{2,1,0:T(8,128)(2,1)}, bf16[1,1584,128]{2,1,0:T(8,128)(2,1)S(1)}, u32[]{:S(2)}, u32[]{:S(2)}) collective-permute-start(bf16[1,1584,128]{2,1,0:T(8,128)(2,1)} %get-tuple-element.25.refs_0_), channel_id=1, source_target_pairs={{32,64},{64,32},{96,128},{128,96},{160,192},{192,160},{33,65},{65,... | collective-permute-start | bytes 1216520 | tf_op jit(solution)/shard_map/ppermute | solution.py:28
  19.1 6.1 %collective-permute-start.2 = (bf16[1,1584,128]{2,1,0:T(8,128)(2,1)}, bf16[1,1584,128]{2,1,0:T(8,128)(2,1)S(1)}, u32[]{:S(2)}, u32[]{:S(2)}) collective-permute-start(bf16[1,1584,128]{2,1,0:T(8,128)(2,1)} %get-tuple-element.25.refs_0_), channel_id=1, source_target_pairs={{0,32},{32,0},{64,96},{96,64},{128,160},{160,128},{192,224},{224,1... | collective-permute-start | bytes 1216520 | tf_op jit(solution)/shard_map/ppermute | solution.py:28
  19.3 14.4 %collective-permute-start.5 = (bf16[2,1584,128]{2,1,0:T(8,128)(2,1)S(1)}, bf16[2,1584,128]{2,1,0:T(8,128)(2,1)S(1)}, u32[]{:S(2)}, u32[]{:S(2)}) collective-permute-start(bf16[2,1584,128]{2,1,0:T(8,128)(2,1)S(1)} %constant_dynamic-update-slice_fusion), channel_id=1, source_target_pairs={{32,64},{64,32},{96,128},{128,96},{160,192},{192,160},{33,65},{65,... | collective-permute-start | bytes 2433032 | tf_op jit(solution)/shard_map/ppermute | solution.py:28
  22.6 11.1 %collective-permute-start.4 = (bf16[2,1584,128]{2,1,0:T(8,128)(2,1)S(1)}, bf16[2,1584,128]{2,1,0:T(8,128)(2,1)S(1)}, u32[]{:S(2)}, u32[]{:S(2)}) collective-permute-start(bf16[2,1584,128]{2,1,0:T(8,128)(2,1)S(1)} %constant_dynamic-update-slice_fusion), channel_id=1, source_target_pairs={{0,32},{32,0},{64,96},{96,64},{128,160},{160,128},{192,224},{224,1... | collective-permute-start | bytes 2433032 | tf_op jit(solution)/shard_map/ppermute | solution.py:28
  46.6 11.5 %collective-permute-start.8 = (bf16[3,256,384]{2,1,0:T(8,128)(2,1)S(1)}, bf16[3,256,384]{2,1,0:T(8,128)(2,1)S(1)}, u32[]{:S(2)}, u32[]{:S(2)}) collective-permute-start(bf16[3,256,384]{2,1,0:T(8,128)(2,1)S(1)} %get-tuple-element.37), channel_id=1, source_target_pairs={{32,64},{64,32},{96,128},{128,96},{160,192},{192,160},{33,65},{65,... | collective-permute-start | bytes 1769480 | tf_op jit(solution)/shard_map/ppermute | solution.py:28
  50.0 8.0 %collective-permute-start.9 = (bf16[3,256,384]{2,1,0:T(8,128)(2,1)S(1)}, bf16[3,256,384]{2,1,0:T(8,128)(2,1)S(1)}, u32[]{:S(2)}, u32[]{:S(2)}) collective-permute-start(bf16[3,256,384]{2,1,0:T(8,128)(2,1)S(1)} %get-tuple-element.38), channel_id=1, source_target_pairs={{0,32},{32,0},{64,96},{96,64},{128,160},{160,128},{192,224},{224,1... | collective-permute-start | bytes 1769480 | tf_op jit(solution)/shard_map/ppermute | solution.py:28
  50.1 19.6 %collective-permute-start.13 = (bf16[2,384,256]{2,1,0:T(8,128)(2,1)S(1)}, bf16[2,384,256]{2,1,0:T(8,128)(2,1)S(1)}, u32[]{:S(2)}, u32[]{:S(2)}) collective-permute-start(bf16[2,384,256]{2,1,0:T(8,128)(2,1)S(1)} %get-tuple-element.43), channel_id=1, source_target_pairs={{1,2},{2,1},{3,4},{4,3},{5,6},{6,5},{9,10},{10,9},{11,12},{12,11},... | collective-permute-start | bytes 1179656 | tf_op jit(solution)/shard_map/ppermute | solution.py:28
  54.0 15.8 %collective-permute-start.12 = (bf16[2,384,256]{2,1,0:T(8,128)(2,1)S(1)}, bf16[2,384,256]{2,1,0:T(8,128)(2,1)S(1)}, u32[]{:S(2)}, u32[]{:S(2)}) collective-permute-start(bf16[2,384,256]{2,1,0:T(8,128)(2,1)S(1)} %get-tuple-element.42), channel_id=1, source_target_pairs={{0,1},{1,0},{2,3},{3,2},{4,5},{5,4},{6,7},{7,6},{8,9},{9,8},{10,11... | collective-permute-start | bytes 1179656 | tf_op jit(solution)/shard_map/ppermute | solution.py:28
  58.3 11.5 %collective-permute-start.11 = (bf16[1,256,384]{2,1,0:T(8,128)(2,1)S(1)}, bf16[1,256,384]{2,1,0:T(8,128)(2,1)S(1)}, u32[]{:S(2)}, u32[]{:S(2)}) collective-permute-start(bf16[1,256,384]{2,1,0:T(8,128)(2,1)S(1)} %get-tuple-element.47), channel_id=1, source_target_pairs={{8,16},{16,8},{9,17},{17,9},{10,18},{18,10},{11,19},{19,11},{12,20... | collective-permute-start | bytes 589832 | tf_op jit(solution)/shard_map/ppermute | solution.py:28
  59.0 19.7 %collective-permute-start.10 = (bf16[1,256,384]{2,1,0:T(8,128)(2,1)S(1)}, bf16[1,256,384]{2,1,0:T(8,128)(2,1)S(1)}, u32[]{:S(2)}, u32[]{:S(2)}) collective-permute-start(bf16[1,256,384]{2,1,0:T(8,128)(2,1)S(1)} %get-tuple-element.48), channel_id=1, source_target_pairs={{0,8},{8,0},{16,24},{24,16},{1,9},{9,1},{17,25},{25,17},{2,10},{10... | collective-permute-start | bytes 589832 | tf_op jit(solution)/shard_map/ppermute | solution.py:28
